TPU v7x, 32 devices: a whole 2x2x4 slice. The times are simulated.
32 devices in a mesh: seq: 16 (over z, y, core), tp: 2 (over x).
Axes of the slice: x: 2, y: 2, z: 4, core: 2. Of those that a mesh axis runs over, the one named last changes fastest.
Arguments:
- inputs: bfloat16 [2, 2048, 2048], P(None, 'seq', 'tp'), may hold values from -6 to 6
- segments: int32 [2, 2048], P(None, 'seq'), may hold values from 0 to 12, as said below
- keys: bfloat16 [2, 2048, 2048], P(None, 'seq', 'tp'), may hold values from -9 to 9
- values: bfloat16 [2, 2048, 2048], P(None, 'seq', 'tp'), may hold values from -6 to 6
- attn_gain: float32 [2048], replicated, may hold values from 0.5 to 1.5
- query_weight: bfloat16 [2048, 2048], P(None, 'tp'), may hold values from -0.125 to 0.125
- out_weight: bfloat16 [2048, 2048], P(None, 'tp'), may hold values from -0.75 to 0.75
- ffn_gain: float32 [2048], replicated, may hold values from 0.5 to 1.5
- gate_weight: bfloat16 [2048, 5504], P(None, 'tp'), may hold values from -0.125 to 0.125
- up_weight: bfloat16 [2048, 5504], P(None, 'tp'), may hold values from -0.125 to 0.125
- down_weight: bfloat16 [2048, 5504], P(None, 'tp'), may hold values from -0.078125 to 0.078125
- cotangent: bfloat16 [2, 2048, 2048], P(None, 'seq', 'tp'), may hold values from -6 to 6
Outputs:
- mixed: bfloat16 [2, 2048, 2048], P(None, 'seq', 'tp')
- input_grad: float32 [2, 2048, 2048], P(None, 'seq', 'tp')
- key_grad: float32 [2, 2048, 2048], P(None, 'seq', 'tp')
- value_grad: float32 [2, 2048, 2048], P(None, 'seq', 'tp')
- attn_gain_grad: float32 [2048], P('seq')
- query_grad: float32 [2048, 2048], P('seq', 'tp')
- out_grad: float32 [2048, 2048], P('seq', 'tp')
- ffn_gain_grad: float32 [2048], P('seq')
- gate_grad: float32 [2048, 5504], P('seq', 'tp')
- up_grad: float32 [2048, 5504], P('seq', 'tp')
- down_grad: float32 [2048, 5504], P('seq', 'tp')
Inputs may be any that keep to these rules, and one draw needn't show every extreme that they name: `segments`: document numbers never fall along a row.
All inputs are finite; a program needn't handle non-finite values.
Results may differ from a plain program's by a relative error of at most 0.02.
Values may be sent and summed in bfloat16 or wider, within the bound.
A program may use at most 448 MiB of HBM per device.

v0:
```python
import math

import jax
import jax.numpy as jnp
from jax import lax
from jax.sharding import PartitionSpec as P

HEAD_DIM = 128
CUTS = 12


EPSILON = 1e-06
NEGATIVE_FILL = -1e30


def inverse_root(stream):
    return lax.rsqrt(jnp.mean(stream * stream, axis=-1, keepdims=True) + EPSILON)


def key_mask(doc_start, query_pos, begin, row_count):
    key_pos = begin + jnp.arange(row_count, dtype=jnp.int32)
    earlier = key_pos[None, None, :] <= query_pos[None, :, None]
    same_doc = key_pos[None, None, :] >= doc_start[:, :, None]
    return (earlier & same_doc)[:, None]


def per_device(
    inputs,
    segments,
    keys,
    values,
    attn_gain,
    query_weight,
    out_weight,
    ffn_gain,
    gate_weight,
    up_weight,
    down_weight,
    cotangent,
):
    batch_rows, local_tokens, half_width = inputs.shape
    local_heads = half_width // HEAD_DIM
    seq_devices = lax.axis_size("seq")
    row_length = local_tokens * seq_devices
    seq_index = lax.axis_index("seq")
    tp_index = lax.axis_index("tp")
    query_scale = HEAD_DIM ** (-0.5)
    bfloat = jnp.bfloat16
    single = jnp.float32
    whole = lax.all_gather(inputs, "tp", axis=2, tiled=True).astype(single)
    root_one = inverse_root(whole)
    scaled_one = whole * root_one
    normed_one = (scaled_one * attn_gain).astype(bfloat)
    query = (
        jnp.einsum("rtd,de->rte", normed_one, query_weight, preferred_element_type=single)
        * query_scale
    ).astype(bfloat)
    query_heads = query.reshape(batch_rows, local_tokens, local_heads, HEAD_DIM)
    bins = jnp.arange(CUTS + 1, dtype=jnp.int32)
    onehot = (segments[:, :, None] == bins[None, None, :]).astype(single)
    totals = lax.psum(jnp.sum(onehot, axis=1), "seq")
    ends = jnp.cumsum(totals, axis=-1)
    before = ends - totals
    doc_start = jnp.sum(onehot * before[:, None, :], axis=-1).astype(jnp.int32)
    query_pos = seq_index * local_tokens + jnp.arange(local_tokens, dtype=jnp.int32)
    first_needed = jnp.min(doc_start)
    last_needed = seq_index * local_tokens + local_tokens - 1
    start_state = (
        jnp.full((batch_rows, local_heads, local_tokens), NEGATIVE_FILL, single),
        jnp.zeros((batch_rows, local_heads, local_tokens), single),
        jnp.zeros((batch_rows, local_heads, local_tokens, HEAD_DIM), single),
    )
    key_piece = lax.all_gather(keys, "seq", axis=1, tiled=True)
    value_piece = lax.all_gather(values, "seq", axis=1, tiled=True)
    piece_rows = key_piece.shape[1]
    fold_key_block = math.gcd(piece_rows, 512)

    def fold_step(block_index, state):
        running_max, running_sum, running_out = state
        begin = block_index * fold_key_block

        def fold_work(unused):
            key_heads = lax.dynamic_slice_in_dim(
                key_piece, block_index * fold_key_block, fold_key_block, 1
            ).reshape(batch_rows, fold_key_block, local_heads, HEAD_DIM)
            value_heads = lax.dynamic_slice_in_dim(
                value_piece, block_index * fold_key_block, fold_key_block, 1
            ).reshape(batch_rows, fold_key_block, local_heads, HEAD_DIM)
            scores = jnp.einsum(
                "rqhe,rkhe->rhqk", query_heads, key_heads, preferred_element_type=single
            )
            allowed = key_mask(doc_start, query_pos, begin, fold_key_block)
            scores = jnp.where(allowed, scores, NEGATIVE_FILL)
            new_max = jnp.maximum(running_max, jnp.max(scores, axis=-1))
            weights = jnp.where(allowed, jnp.exp(scores - new_max[..., None]), 0.0)
            decay = jnp.exp(running_max - new_max)
            new_sum = running_sum * decay + jnp.sum(weights, axis=-1)
            new_out = running_out * decay[..., None] + jnp.einsum(
                "rhqk,rkhe->rhqe",
                weights.astype(bfloat),
                value_heads,
                preferred_element_type=single,
            )
            return (new_max, new_sum, new_out)

        def keep_state(unused):
            return (running_max, running_sum, running_out)

        needed = (begin <= last_needed) & (begin + fold_key_block - 1 >= first_needed)
        return lax.cond(needed, fold_work, keep_state, 0)

    running_max, running_sum, running_out = lax.fori_loop(
        0, piece_rows // fold_key_block, fold_step, start_state
    )
    log_total = running_max + jnp.log(running_sum)
    attended = running_out / running_sum[..., None]
    attended_low = (
        attended.transpose(0, 2, 1, 3).reshape(batch_rows, local_tokens, half_width).astype(bfloat)
    )
    branch = jnp.einsum("rth,dh->rtd", attended_low, out_weight, preferred_element_type=single)
    middle = whole + lax.psum(branch.astype(jnp.bfloat16), "tp").astype(jnp.float32)
    middle_share = lax.dynamic_slice_in_dim(middle, tp_index * half_width, half_width, 2)
    root_two = inverse_root(middle)
    scaled_two = middle * root_two
    normed_two = (scaled_two * ffn_gain).astype(bfloat)
    gate = jnp.einsum("rtd,df->rtf", normed_two, gate_weight, preferred_element_type=single)
    up_proj = jnp.einsum("rtd,df->rtf", normed_two, up_weight, preferred_element_type=single)
    sigma = jax.nn.sigmoid(gate)
    activated = gate * sigma
    hidden = (activated * up_proj).astype(bfloat)
    ffn_part = jnp.einsum("rtf,df->rtd", hidden, down_weight, preferred_element_type=single)
    output = (
        middle_share
        + lax.psum_scatter(
            ffn_part.astype(jnp.bfloat16), "tp", scatter_dimension=2, tiled=True
        ).astype(jnp.float32)
    ).astype(bfloat)
    grad_out = lax.all_gather(cotangent, "tp", axis=2, tiled=True)
    d_hidden = jnp.einsum("rtd,df->rtf", grad_out, down_weight, preferred_element_type=single)
    d_gate = (d_hidden * up_proj * sigma * (1.0 + gate * (1.0 - sigma))).astype(bfloat)
    d_up = (d_hidden * activated).astype(bfloat)
    d_two_part = jnp.einsum(
        "rtf,df->rtd", d_gate, gate_weight, preferred_element_type=single
    ) + jnp.einsum("rtf,df->rtd", d_up, up_weight, preferred_element_type=single)
    d_two = lax.psum(d_two_part.astype(jnp.bfloat16), "tp").astype(jnp.float32)
    gained_two = d_two * ffn_gain
    d_middle = (
        grad_out.astype(single)
        + root_two * gained_two
        - middle * root_two**3 * jnp.mean(gained_two * middle, axis=-1, keepdims=True)
    )
    normed_rows = normed_two
    gate_term = jnp.einsum("rtd,rtf->df", normed_rows, d_gate, preferred_element_type=single)
    up_term = jnp.einsum("rtd,rtf->df", normed_rows, d_up, preferred_element_type=single)
    down_term = jnp.einsum("rtd,rtf->df", grad_out, hidden, preferred_element_type=single)
    gain_term = jnp.sum(d_two * scaled_two, axis=(0, 1))
    gate_grad, up_grad, down_grad, ffn_gain_grad = lax.psum_scatter(
        (gate_term, up_term, down_term, gain_term), "seq", scatter_dimension=0, tiled=True
    )
    error = d_middle.astype(bfloat)
    d_attended = jnp.einsum("rtd,dh->rth", error, out_weight, preferred_element_type=single).astype(
        bfloat
    )
    d_heads = d_attended.reshape(batch_rows, local_tokens, local_heads, HEAD_DIM)
    carried = jnp.einsum("rqhe,rhqe->rhq", d_heads.astype(single), attended)
    key_all, value_all = (
        lax.all_gather(keys, "seq", axis=1, tiled=True),
        lax.all_gather(values, "seq", axis=1, tiled=True),
    )
    key_block = math.gcd(row_length, 512)

    def block_terms(begin):
        key_heads = lax.dynamic_slice_in_dim(key_all, begin, key_block, 1).reshape(
            batch_rows, key_block, local_heads, HEAD_DIM
        )
        value_heads = lax.dynamic_slice_in_dim(value_all, begin, key_block, 1).reshape(
            batch_rows, key_block, local_heads, HEAD_DIM
        )
        scores = jnp.einsum(
            "rqhe,rkhe->rhqk", query_heads, key_heads, preferred_element_type=single
        )
        allowed = key_mask(doc_start, query_pos, begin, key_block)
        probs = jnp.where(
            allowed, jnp.exp(jnp.where(allowed, scores, NEGATIVE_FILL) - log_total[..., None]), 0.0
        )
        d_probs = jnp.einsum("rqhe,rkhe->rhqk", d_heads, value_heads, preferred_element_type=single)
        d_scores = (probs * (d_probs - carried[..., None])).astype(bfloat)
        query_part = jnp.einsum(
            "rhqk,rkhe->rhqe", d_scores, key_heads, preferred_element_type=single
        )
        return (probs, d_scores, query_part)

    query_zero = jnp.zeros((batch_rows, local_heads, local_tokens, HEAD_DIM), single)

    def back_step(block_index, state):
        d_query, key_terms, value_terms = state
        begin = block_index * key_block

        def back_work(unused):
            probs, d_scores, query_part = block_terms(begin)
            value_part = jnp.einsum(
                "rhqk,rqhe->rkhe", probs.astype(bfloat), d_heads, preferred_element_type=single
            )
            key_part = jnp.einsum(
                "rhqk,rqhe->rkhe", d_scores, query_heads, preferred_element_type=single
            )
            return (
                query_part,
                key_part.reshape(batch_rows, key_block, half_width),
                value_part.reshape(batch_rows, key_block, half_width),
            )

        def skip_block(unused):
            empty_rows = jnp.zeros((batch_rows, key_block, half_width), single)
            return (jnp.zeros_like(d_query), empty_rows, empty_rows)

        needed = (begin <= last_needed) & (begin + key_block - 1 >= first_needed)
        query_part, key_part, value_part = lax.cond(needed, back_work, skip_block, 0)
        return (
            d_query + query_part,
            lax.dynamic_update_slice_in_dim(key_terms, key_part, begin, 1),
            lax.dynamic_update_slice_in_dim(value_terms, value_part, begin, 1),
        )

    back_start = (
        query_zero,
        jnp.zeros((batch_rows, row_length, half_width), single),
        jnp.zeros((batch_rows, row_length, half_width), single),
    )
    d_query, key_terms, value_terms = lax.fori_loop(
        0, row_length // key_block, back_step, back_start
    )
    key_grad, value_grad = (
        lax.psum_scatter(key_terms, "seq", scatter_dimension=1, tiled=True),
        lax.psum_scatter(value_terms, "seq", scatter_dimension=1, tiled=True),
    )
    d_query_rows = (
        d_query.transpose(0, 2, 1, 3).reshape(batch_rows, local_tokens, half_width).astype(bfloat)
    )
    d_one_part = (
        jnp.einsum("rte,de->rtd", d_query_rows, query_weight, preferred_element_type=single)
        * query_scale
    )
    d_one = lax.psum(d_one_part.astype(jnp.bfloat16), "tp").astype(jnp.float32)
    gained_one = d_one * attn_gain
    d_whole = (
        d_middle
        + root_one * gained_one
        - whole * root_one**3 * jnp.mean(gained_one * whole, axis=-1, keepdims=True)
    )
    input_grad = lax.dynamic_slice_in_dim(d_whole, tp_index * half_width, half_width, 2)
    normed_rows = normed_one
    query_term = (
        jnp.einsum("rtd,rte->de", normed_rows, d_query_rows, preferred_element_type=single)
        * query_scale
    )
    out_term = jnp.einsum("rtd,rth->dh", error, attended_low, preferred_element_type=single)
    gain_term = jnp.sum(d_one * scaled_one, axis=(0, 1))
    query_grad, out_grad, attn_gain_grad = lax.psum_scatter(
        (query_term, out_term, gain_term), "seq", scatter_dimension=0, tiled=True
    )
    return (
        output,
        input_grad,
        key_grad,
        value_grad,
        attn_gain_grad,
        query_grad,
        out_grad,
        ffn_gain_grad,
        gate_grad,
        up_grad,
        down_grad,
    )


def solution(mesh):
    in_specs = (
        P(None, "seq", "tp"),
        P(None, "seq"),
        P(None, "seq", "tp"),
        P(None, "seq", "tp"),
        P(),
        P(None, "tp"),
        P(None, "tp"),
        P(),
        P(None, "tp"),
        P(None, "tp"),
        P(None, "tp"),
        P(None, "seq", "tp"),
    )
    out_specs = (
        P(None, "seq", "tp"),
        P(None, "seq", "tp"),
        P(None, "seq", "tp"),
        P(None, "seq", "tp"),
        P("seq"),
        P("seq", "tp"),
        P("seq", "tp"),
        P("seq"),
        P("seq", "tp"),
        P("seq", "tp"),
        P("seq", "tp"),
    )
    return jax.shard_map(
        per_device, mesh=mesh, in_specs=in_specs, out_specs=out_specs, check_vma=False
    )
```

profile of v0, /device:TPU:0, one launch (start us, length us, event | category | flops | bytes accessed | tf_op | source)
XLA Modules:
  0.0 1821.4 jit_solution(12407670048944130353)
XLA Ops:
  12.9 35.5 %psum.28 = f32[2,13]{0,1:T(8,128)S(1)} all-reduce(f32[2,13]{0,1:T(8,128)S(1)} %convert_reduce_fusion), channel_id=1, replica_groups=mesh['seq'=16,'tp'=2] {'seq'}, use_global_device_ids=true, to_apply=%region_1.0 | all-reduce | flops 26 | bytes 208 | tf_op jit(solution)/shard_map/psum | solution.py:61
  55.8 58.7 %all-gather.7.cloned.1.call-done = bf16[2,2048,1024]{1,2,0:T(8,128)(2,1)} async-done(((bf16[2,128,1024]{1,2,0:T(8,128)(2,1)}), bf16[2,2048,1024]{1,2,0:T(8,128)(2,1)}) %all-gather.7.cloned.1.call-update) | async-done | bytes 8388624 | tf_op jit(solution)/shard_map/all_gather | solution.py:73
  114.5 79.0 %all-gather.9.cloned.1.call-done = bf16[2,2048,1024]{1,2,0:T(8,128)(2,1)} async-done(((bf16[2,128,1024]{1,2,0:T(8,128)(2,1)}), bf16[2,2048,1024]{1,2,0:T(8,128)(2,1)}) %all-gather.9.cloned.1.call-update) | async-done | bytes 8388624 | tf_op jit(solution)/shard_map/all_gather | solution.py:74
  193.6 9.1 while.44
  194.3 6.4 conditional.6
  204.1 4.5 fusion.61
  208.9 5.5 all-gather.11.cloned.1.call-done
  214.4 7.4 fusion.31
  221.8 44.6 %all-reduce.7.cloned.1.call-done = bf16[2,128,2048]{2,1,0:T(8,128)(2,1)} async-done(((bf16[2,128,2048]{2,1,0:T(8,128)(2,1)}), bf16[2,128,2048]{2,1,0:T(8,128)(2,1)}) %all-reduce.7.cloned.1.call-update) | async-done | bytes 1048592 | tf_op jit(solution)/shard_map/psum | solution.py:121
  268.7 8.0 fusion.37
  276.7 13.4 multiply_convert_fusion.1
  293.4 4.1 fusion.64
  297.6 8.8 fusion.67
  306.9 30.8 %all-reduce.9.cloned.1.call-done = bf16[2,128,2048]{2,1,0:T(8,128)(2,1)} async-done(((bf16[2,128,2048]{2,1,0:T(8,128)(2,1)}), bf16[2,128,2048]{2,1,0:T(8,128)(2,1)}) %all-reduce.9.cloned.1.call-update) | async-done | bytes 1048592 | tf_op jit(solution)/shard_map/psum | solution.py:145
  353.3 8.0 broadcast.165.clone
  361.3 8.0 broadcast.165.clone2
  369.3 115.2 %while.45 = (s32[]{:T(128)}, f32[2,8,128,128]{3,2,1,0:T(8,128)}, f32[2,2048,1024]{2,1,0:T(8,128)}, f32[2,2048,1024]{2,1,0:T(8,128)}, s32[]{:T(128)}, /*index=5*/...) while((s32[]{:T(128)}, f32[2,8,128,128]{3,2,1,0:T(8,128)}, ...), condition=%wide.region_20.21_spmd.clone, body=%wide.region_17.20_spmd.clone.sunk | while | flops 1353515648 | bytes 82347440 | solution.py:230
  370.1 12.2 conditional.7
  383.3 5.4 copy.155
  388.7 5.4 copy.156
  394.1 8.4 constant_dynamic-update-slice_fusion.3
  403.1 5.1 conditional.7
  410.6 5.4 copy.155
  416.0 5.4 copy.156
  421.4 8.6 constant_dynamic-update-slice_fusion.3
  430.5 5.1 conditional.7
  438.0 5.4 copy.155
  443.4 5.4 copy.156
  448.8 8.4 constant_dynamic-update-slice_fusion.3
  457.8 5.1 conditional.7
  465.3 5.4 copy.155
  470.6 5.4 copy.156
  476.1 8.4 constant_dynamic-update-slice_fusion.3
  486.0 4.5 fusion.58
  490.6 4.7 bitcast_multiply_fusion.1
  496.9 5.6 convolution_bitcast_fusion.3
  503.8 10.6 convolution_bitcast_fusion.1
  514.5 10.6 convolution_bitcast_fusion
  525.2 10.6 convolution_bitcast_fusion.2
  541.7 10.0 all-reduce.11.cloned.1.call-done
  555.1 74.8 %all-reduce.2 = (f32[2048]{0:T(1024)S(1)}, f32[2048]{0:T(1024)S(1)}) all-reduce(f32[2048]{0:T(1024)S(1)} %get-tuple-element.1076, f32[2048]{0:T(1024)S(1)} %copy-done.15), channel_id=5, replica_groups=mesh['seq'=16,'tp'=2] {'seq'}, use_global_device_ids=true, to_apply=%region_26.27.clone | all-reduce | flops 4096 | bytes 32768
  633.8 27.7 %reduce-scatter.15.cloned.1.call-done = f32[128,1024]{1,0:T(8,128)} async-done(((f32[2048,1024]{1,0:T(8,128)}), f32[128,1024]{1,0:T(8,128)}) %reduce-scatter.15.cloned.1.call-update) | async-done | bytes 524304 | tf_op jit(solution)/shard_map/reduce_scatter | solution.py:259
  661.5 109.0 %reduce-scatter.17.cloned.1.call-done = f32[128,1024]{1,0:T(8,128)} async-done(((f32[2048,1024]{1,0:T(8,128)}), f32[128,1024]{1,0:T(8,128)}) %reduce-scatter.17.cloned.1.call-update) | async-done | bytes 524304 | tf_op jit(solution)/shard_map/reduce_scatter | solution.py:259
  770.4 183.0 %reduce-scatter.11.cloned.1.call-done = f32[2,128,1024]{2,1,0:T(8,128)} async-done(((f32[2,2048,1024]{2,1,0:T(8,128)}), f32[2,128,1024]{2,1,0:T(8,128)}) %reduce-scatter.11.cloned.1.call-update) | async-done | bytes 1048592 | tf_op jit(solution)/shard_map/reduce_scatter | solution.py:234
  953.5 182.1 %reduce-scatter.13.cloned.1.call-done = f32[2,128,1024]{2,1,0:T(8,128)} async-done(((f32[2,2048,1024]{2,1,0:T(8,128)}), f32[2,128,1024]{2,1,0:T(8,128)}) %reduce-scatter.13.cloned.1.call-update) | async-done | bytes 1048592 | tf_op jit(solution)/shard_map/reduce_scatter | solution.py:235
  1135.6 226.4 %reduce-scatter.19.cloned.1.call-done = f32[128,2752]{0,1:T(8,128)} async-done(((f32[2048,2752]{0,1:T(8,128)}), f32[128,2752]{0,1:T(8,128)}) %reduce-scatter.19.cloned.1.call-update) | async-done | bytes 1409040 | tf_op jit(solution)/shard_map/reduce_scatter | solution.py:157
  1362.0 226.4 %reduce-scatter.21.cloned.1.call-done = f32[128,2752]{0,1:T(8,128)} async-done(((f32[2048,2752]{0,1:T(8,128)}), f32[128,2752]{0,1:T(8,128)}) %reduce-scatter.21.cloned.1.call-update) | async-done | bytes 1409040 | tf_op jit(solution)/shard_map/reduce_scatter | solution.py:157
  1588.3 226.3 %reduce-scatter.23.cloned.1.call-done = f32[128,2752]{0,1:T(8,128)} async-done(((f32[2048,2752]{0,1:T(8,128)}), f32[128,2752]{0,1:T(8,128)}) %reduce-scatter.23.cloned.1.call-update) | async-done | bytes 1409040 | tf_op jit(solution)/shard_map/reduce_scatter | solution.py:157
  (178 shorter events, 95.1 us)
Async XLA Ops:
  7.2 5.6 copy-start.19
  7.2 44.1 %copy-start.12 = (f32[2048]{0:T(1024)S(1)}, f32[2048]{0:T(1024)}, u32[]{:S(2)}) copy-start(f32[2048]{0:T(1024)} %param.24) | copy-start | bytes 24580
  7.2 42.1 %all-gather.5.cloned.1.call-start = ((), (), s32[]{:S(2)}) async-start(), calls=%async_computation.8 | async-start | bytes 1572864 | tf_op jit(solution)/shard_map/all_gather | solution.py:50
  7.9 106.5 %all-gather.7.cloned.1.call-start = ((), (), s32[]{:S(2)}) async-start(), calls=%async_computation.9 | async-start | bytes 8912896 | tf_op jit(solution)/shard_map/all_gather | solution.py:73
  10.0 183.5 %all-gather.9.cloned.1.call-start = ((), (), s32[]{:S(2)}) async-start(), calls=%async_computation.10 | async-start | bytes 8912896 | tf_op jit(solution)/shard_map/all_gather | solution.py:74
  12.2 202.3 %all-gather.11.cloned.1.call-start = ((), (), s32[]{:S(2)}) async-start(), calls=%async_computation.13 | async-start | bytes 1572864 | tf_op jit(solution)/shard_map/all_gather | solution.py:138
  12.7 253.7 %all-reduce.7.cloned.1.call-start = ((), (), s32[]{:S(2)}) async-start(), calls=%async_computation.11 | async-start | bytes 2097152 | tf_op jit(solution)/shard_map/psum | solution.py:121
  51.3 3.8 copy-start.16
  203.1 5.5 copy-start.6
  203.2 0.9 copy-start.11
  208.6 57.8 %copy-start = (bf16[2,128,2048]{2,1,0:T(8,128)(2,1)S(1)}, bf16[2,128,2048]{2,1,0:T(8,128)(2,1)}, u32[]{:S(2)}) copy-start(bf16[2,128,2048]{2,1,0:T(8,128)(2,1)} %all-gather.5.cloned.1.call-done) | copy-start | bytes 3145732
  208.6 59.5 %copy-start.14 = (f32[2048]{0:T(1024)S(1)}, f32[2048]{0:T(1024)}, u32[]{:S(2)}) copy-start(f32[2048]{0:T(1024)} %param.27) | copy-start | bytes 24580
  208.6 129.1 %all-reduce.9.cloned.1.call-start = ((), (), s32[]{:S(2)}) async-start(), calls=%async_computation.14 | async-start | bytes 2097152 | tf_op jit(solution)/shard_map/psum | solution.py:145
  266.4 1.8 copy-start.3
  268.7 8.0 copy-start.5
  268.7 21.4 %slice-start = ((s8[11272192]{0:T(1024)(128)(4,1)}), s8[4194304]{0:T(1024)(128)(4,1)S(1)}, s32[]{:S(2)}) async-start(s8[11272192]{0:T(1024)(128)(4,1)} %bitcast.154), calls=%async_computation.23 | async-start | bytes 8388608
  276.7 13.5 slice-start.1
  276.7 13.5 slice-start.2
  276.7 16.7 slice-start.3
  276.7 16.7 slice-start.4
  290.1 3.2 copy-start.4
  290.1 3.2 copy-start.8
  290.2 3.2 slice-start.5
  297.5 241.8 %reduce-scatter.9.cloned.1.call-start = ((), (), s32[]{:S(2)}) async-start(), calls=%async_computation.12 | async-start | bytes 1572864 | tf_op jit(solution)/shard_map/reduce_scatter | solution.py:134
  306.4 245.4 %all-reduce.11.cloned.1.call-start = ((), (), s32[]{:S(2)}) async-start(), calls=%async_computation.15 | async-start | bytes 2097152 | tf_op jit(solution)/shard_map/psum | solution.py:244
  337.8 2.9 copy-start.9
  337.8 2.9 copy-start.10
  340.6 2.9 copy-start.20
  342.8 2.1 copy-start.1
  344.8 7.0 copy-start.7
  486.0 4.6 copy-start.13
  486.0 4.6 copy-start.17
  490.5 171.0 %reduce-scatter.15.cloned.1.call-start = ((), (), s32[]{:S(2)}) async-start(), calls=%async_computation.18 | async-start | bytes 8912896 | tf_op jit(solution)/shard_map/reduce_scatter | solution.py:259
  495.3 1.6 copy-start.2
  495.3 275.1 %reduce-scatter.17.cloned.1.call-start = ((), (), s32[]{:S(2)}) async-start(), calls=%async_computation.19 | async-start | bytes 8912896 | tf_op jit(solution)/shard_map/reduce_scatter | solution.py:259
  502.5 451.0 %reduce-scatter.11.cloned.1.call-start = ((), (), s32[]{:S(2)}) async-start(), calls=%async_computation.16 | async-start | bytes 17825792 | tf_op jit(solution)/shard_map/reduce_scatter | solution.py:234
  503.2 632.4 %reduce-scatter.13.cloned.1.call-start = ((), (), s32[]{:S(2)}) async-start(), calls=%async_computation.17 | async-start | bytes 17825792 | tf_op jit(solution)/shard_map/reduce_scatter | solution.py:235
  503.8 858.2 %reduce-scatter.19.cloned.1.call-start = ((), (), s32[]{:S(2)}) async-start(), calls=%async_computation.20 | async-start | bytes 23953408 | tf_op jit(solution)/shard_map/reduce_scatter | solution.py:157
  514.5 1073.9 %reduce-scatter.21.cloned.1.call-start = ((), (), s32[]{:S(2)}) async-start(), calls=%async_computation.21 | async-start | bytes 23953408 | tf_op jit(solution)/shard_map/reduce_scatter | solution.py:157
  525.2 1289.5 %reduce-scatter.23.cloned.1.call-start = ((), (), s32[]{:S(2)}) async-start(), calls=%async_computation.22 | async-start | bytes 23953408 | tf_op jit(solution)/shard_map/reduce_scatter | solution.py:157
  535.8 0.7 copy-start.21
  539.3 15.8 copy-start.15
  539.3 91.7 %copy-start.18 = (f32[2,128]{1,0:T(2,128)S(1)}, f32[2,128]{1,0:T(2,128)}, u32[]{:S(2)}) copy-start(f32[2,128]{1,0:T(2,128)} %get-tuple-element.1146) | copy-start | bytes 3076
Sparse Core Ops, SparseCore 0:
  9.6 23.9 all-gather.4
  36.3 78.0 all-gather.6
  117.2 76.2 all-gather.8
  194.9 19.4 all-gather.10
  217.1 49.2 all-reduce.6
  297.7 40.0 all-reduce.8
  340.6 20.3 reduce-scatter.8
  490.6 61.0 all-reduce.10
  556.4 105.0 reduce-scatter.14
  666.0 104.4 reduce-scatter.16
  775.1 178.2 reduce-scatter.10
  958.0 177.5 reduce-scatter.12
  1140.4 221.5 reduce-scatter.18
  1366.6 221.6 reduce-scatter.20
  1593.0 221.6 reduce-scatter.22
where the time goes:
time: 1830 us; the launch traced here: 1820 us
  waiting for transfers between devices  1410 us (77%)
  local copies, waits for them, and re-layouts  130 us (7%)
  matrix products  113 us (6%)
  blocking collectives  110 us (6%)
  other arithmetic  33.4 us (2%)
    reduce_scatter x3, waiting for transfers between devices, per_device(): lax.psum_scatter((gate_term, up_term, down_term, gain_term), 'seq', scatt...  679 us
    reduce_scatter x1, waiting for transfers between devices, per_device(): lax.psum_scatter(key_terms, 'seq', scatter_dimension=1, tiled=True)  183 us
    reduce_scatter x1, waiting for transfers between devices, per_device(): lax.psum_scatter(value_terms, 'seq', scatter_dimension=1, tiled=True)  182 us
    reduce_scatter x2, waiting for transfers between devices, per_device(): lax.psum_scatter((query_term, out_term, gain_term), 'seq', scatter_dimens...  137 us
    all_gather x1, waiting for transfers between devices, per_device(): value_piece = lax.all_gather(values, 'seq', axis=1, tiled=True)  79 us
    unnamed x1, blocking collectives  74.8 us
    all_gather x1, waiting for transfers between devices, per_device(): key_piece = lax.all_gather(keys, 'seq', axis=1, tiled=True)  58.7 us
    dynamic_update_slice x8, local copies, waits for them, and re-layouts, back_step(): lax.dynamic_update_slice_in_dim(value_terms, value_part, begin, 1)  55.3 us
  transfers between devices with their start and end apart: 15, of which 13 were waited for; matrix products, arithmetic and copies ran while one was open for 13% of the time, Pallas kernels for 0%

commit v1 on v0

--- a/solution.py
+++ b/solution.py
@@ -1,8 +1,11 @@
+import functools
 import math
 
 import jax
 import jax.numpy as jnp
 from jax import lax
+from jax.experimental import pallas as pl
+from jax.experimental.pallas import tpu as pltpu
 from jax.sharding import PartitionSpec as P
 
 HEAD_DIM = 128
@@ -11,6 +14,944 @@
 
 EPSILON = 1e-06
 NEGATIVE_FILL = -1e30
+
+MESH = pl.DeviceIdType.MESH
+BF = jnp.bfloat16
+F32 = jnp.float32
+MIB = 1 << 20
+PLANE = 4
+LANE = 128
+
+
+def dot_nn(a, b):
+    return lax.dot_general(a, b, (((1,), (0,)), ((), ())), preferred_element_type=F32)
+
+
+def dot_nt(a, b):
+    return lax.dot_general(a, b, (((1,), (1,)), ((), ())), preferred_element_type=F32)
+
+
+def dot_tn(a, b):
+    return lax.dot_general(a, b, (((0,), (0,)), ((), ())), preferred_element_type=F32)
+
+
+def aligned(index, size):
+    return pl.ds(pl.multiple_of(index * size, size), size)
+
+
+class Place:
+    def __init__(self, n):
+        self.n = n
+        self.s = lax.axis_index("seq")
+        self.t = lax.axis_index("tp")
+        self.z = self.s // PLANE
+        self.p = lax.rem(self.s, PLANE)
+        self.y = self.p // 2
+        self.c = lax.rem(self.p, 2)
+        base = self.z * PLANE
+        self.core_p = self.y * 2 + 1 - self.c
+        self.side_p = (1 - self.y) * 2 + self.c
+        self.cross_p = (1 - self.y) * 2 + 1 - self.c
+        self.core = (base + self.core_p, self.t)
+        self.side = (base + self.side_p, self.t)
+        self.cross = (base + self.cross_p, self.t)
+        self.twin = (self.s, 1 - self.t)
+
+    def other(self, k):
+        return lax.rem(self.s + k, self.n)
+
+    def enter(self):
+        barrier = pltpu.get_barrier_semaphore()
+
+        def greet(k, unused):
+            pl.semaphore_signal(barrier, inc=1, device_id=(self.other(k), self.t), device_id_type=MESH)
+            return unused
+
+        lax.fori_loop(1, self.n, greet, 0)
+        pl.semaphore_signal(barrier, inc=1, device_id=self.twin, device_id_type=MESH)
+        pl.semaphore_wait(barrier, self.n)
+
+
+def remote(src, dst, send, recv, device):
+    return pltpu.make_async_remote_copy(
+        src_ref=src, dst_ref=dst, send_sem=send, recv_sem=recv, device_id=device, device_id_type=MESH
+    )
+
+
+class Spread:
+    def __init__(self, place, src, dst, send, recv, local):
+        self.place, self.src, self.dst, self.send, self.recv, self.local = place, src, dst, send, recv, local
+
+    def copy(self, k):
+        place = self.place
+        d = place.other(k)
+        return remote(self.src(d), self.dst(), self.send.at[k], self.recv.at[k], (d, place.t))
+
+    def own(self):
+        return pltpu.make_async_copy(self.src(self.place.s), self.dst(), self.local)
+
+    def start(self):
+        self.own().start()
+
+        def one(k, unused):
+            self.copy(k).start()
+            return unused
+
+        lax.fori_loop(1, self.place.n, one, 0)
+
+    def start_to(self, d, unused):
+        k = lax.rem(d - self.place.s + self.place.n, self.place.n)
+
+        @pl.when(k == 0)
+        def _():
+            self.own().start()
+
+        @pl.when(k != 0)
+        def _():
+            self.copy(k).start()
+
+        return unused
+
+    def wait(self):
+        self.own().wait()
+
+        def one(k, unused):
+            self.copy(k).wait()
+            return unused
+
+        lax.fori_loop(1, self.place.n, one, 0)
+
+
+def attention_masks(seg_all, seg_row, seg_col, n, tok):
+    def one(i, unused):
+        piece = seg_all[i]
+        seg_row[:, aligned(i, tok)] = piece
+        seg_col[aligned(i, tok), :] = jnp.transpose(jnp.broadcast_to(piece, (tok, tok)))
+        return unused
+
+    lax.fori_loop(0, n, one, 0)
+
+
+def readable(seg_col, seg_row, key_block, query_block, block):
+    key_seg = seg_col[aligned(key_block, block), :]
+    key_seg = jnp.concatenate([key_seg] * (block // LANE), axis=1)
+    query_seg = seg_row[:, aligned(query_block, block)]
+    key_pos = key_block * block + lax.broadcasted_iota(jnp.int32, (block, block), 0)
+    query_pos = query_block * block + lax.broadcasted_iota(jnp.int32, (block, block), 1)
+    return (key_seg == query_seg) & (key_pos <= query_pos)
+
+
+def forward_kernel(
+    geo,
+    x_in, cot_in, key_in, value_in, seg_in, gain_one, gain_two, wq_in, wo_in,
+    x_all, cot_all, left_cot, middle, normed_two, left_two, attended, unit_q, unit_k, unit_v, unit_o, lse, seg_all,
+    wq, wo, normed_one, query, value_t, seg_row, seg_col, part, part_in, cot_split,
+    tp_s, tp_r, a_s, a_r, br_s, br_r, l_s, l_r, loc,
+):
+    n, rows, tok, width, half, heads, length = geo
+    place = Place(n)
+    s, t = place.s, place.t
+    place.enter()
+    row_s, head_s = s // heads, lax.rem(s, heads)
+    half_at = aligned(t, half)
+
+    to_x = remote(x_in, x_all.at[:, half_at], tp_s.at[0], tp_r.at[0], place.twin)
+    to_x.start()
+    own_x = pltpu.make_async_copy(x_in, x_all.at[:, half_at], loc.at[0])
+    own_x.start()
+    load_q = pltpu.make_async_copy(wq_in, wq, loc.at[1])
+    load_q.start()
+
+    def piece(ref):
+        return lambda d: ref.at[aligned(d // heads, tok), aligned(lax.rem(d, heads), HEAD_DIM)]
+
+    keys = Spread(place, piece(key_in), lambda: unit_k.at[aligned(s, tok), :], a_s.at[0], a_r.at[0], loc.at[2])
+    vals = Spread(place, piece(value_in), lambda: unit_v.at[aligned(s, tok), :], a_s.at[1], a_r.at[1], loc.at[3])
+    segs = Spread(place, lambda d: seg_in.at[d // heads], lambda: seg_all.at[s], a_s.at[2], a_r.at[2], loc.at[4])
+    qrys = Spread(place, piece(query), lambda: unit_q.at[aligned(s, tok), :], a_s.at[3], a_r.at[3], loc.at[5])
+    segs.start()
+    keys.start()
+    vals.start()
+    to_cot = remote(cot_in, cot_all.at[:, half_at], tp_s.at[1], tp_r.at[1], place.twin)
+    to_cot.start()
+    own_cot = pltpu.make_async_copy(cot_in, cot_all.at[:, half_at], loc.at[6])
+    own_cot.start()
+    load_o = pltpu.make_async_copy(wo_in, wo, loc.at[7])
+    load_o.start()
+
+    own_x.wait()
+    to_x.wait()
+    step = 64
+
+    def norm_one(i, unused):
+        at = aligned(i, step)
+        x = x_all[at, :].astype(F32)
+        root = lax.rsqrt(jnp.mean(x * x, axis=-1, keepdims=True) + EPSILON)
+        normed_one[at, :] = (x * root * gain_one[...]).astype(BF)
+        return unused
+
+    lax.fori_loop(0, rows * tok // step, norm_one, 0)
+    load_q.wait()
+    query[...] = (dot_nn(normed_one[...], wq[...]) * HEAD_DIM ** (-0.5)).astype(BF)
+    qrys.start()
+
+    segs.wait()
+    attention_masks(seg_all, seg_row, seg_col, n, tok)
+    keys.wait()
+    vals.wait()
+
+    def turn(i, unused):
+        at = aligned(i, tok)
+        value_t[:, at] = jnp.transpose(unit_v[at, :].astype(F32)).astype(BF)
+        return unused
+
+    lax.fori_loop(0, n, turn, 0)
+    qrys.wait()
+
+    back = Spread(
+        place,
+        lambda d: unit_o.at[aligned(d, tok), :],
+        lambda: attended.at[aligned(row_s, tok), aligned(head_s, HEAD_DIM)],
+        a_s.at[4], a_r.at[4], loc.at[8],
+    )
+    block = 512
+    owners = block // tok
+
+    def query_step(qi, unused):
+        query_block = unit_q[aligned(qi, block), :]
+
+        def key_step(j, carry):
+            top, total, acc = carry
+            kj = qi - j
+            scores = dot_nt(unit_k[aligned(kj, block), :], query_block)
+            scores = jnp.where(readable(seg_col, seg_row, kj, qi, block), scores, NEGATIVE_FILL)
+            new_top = jnp.maximum(top, jnp.max(scores, axis=0, keepdims=True))
+            weights = jnp.exp(scores - new_top)
+            decay = jnp.exp(top - new_top)
+            total = total * decay + jnp.sum(weights, axis=0, keepdims=True)
+            acc = acc * decay + dot_nn(value_t[:, aligned(kj, block)], weights.astype(BF))
+            return new_top, total, acc
+
+        start = (
+            jnp.full((1, block), NEGATIVE_FILL, F32),
+            jnp.zeros((1, block), F32),
+            jnp.zeros((HEAD_DIM, block), F32),
+        )
+        top, total, acc = lax.fori_loop(0, qi + 1, key_step, start)
+        lse[:, aligned(qi, block)] = top + jnp.log(total)
+        unit_o[aligned(qi, block), :] = jnp.transpose(acc / total).astype(BF)
+
+        return lax.fori_loop(qi * owners, (qi + 1) * owners, back.start_to, unused)
+
+    lax.fori_loop(0, length // block, query_step, 0)
+
+    own_cot.wait()
+    to_cot.wait()
+    split_rows(cot_all, cot_split, n)
+    plane_cot = Plane(place, cot_split, left_cot, l_s, l_r, loc.at[9], rows * tok)
+    plane_cot.start()
+    load_o.wait()
+    back.wait()
+
+    chunks = part.shape[0]
+    wide = width // chunks
+
+    def to_twin(i):
+        return remote(part.at[i], part_in.at[i], br_s.at[i], br_r.at[i], place.twin)
+
+    def project(i, unused):
+        part[i] = dot_nt(attended[...], wo[aligned(i, wide), :]).astype(BF)
+        to_twin(i).start()
+        return unused
+
+    lax.fori_loop(0, chunks, project, 0)
+    plane_cot.forward()
+
+    def add(i, square):
+        to_twin(i).wait()
+        at = aligned(i, wide)
+        both = part[i].astype(F32) + part_in[i].astype(F32)
+        mid = x_all[:, at].astype(F32) + both
+        middle[:, at] = mid
+        return square + jnp.sum(mid * mid, axis=-1, keepdims=True)
+
+    square = lax.fori_loop(0, chunks, add, jnp.zeros((rows * tok, 1), F32))
+    root_two = lax.rsqrt(square * (1.0 / width) + EPSILON)
+
+    def norm_two(i, unused):
+        at = aligned(i, wide)
+        normed_two[:, at] = (middle[:, at] * root_two * gain_two[:, at]).astype(BF)
+        return unused
+
+    lax.fori_loop(0, chunks, norm_two, 0)
+    split_rows(normed_two, left_two, n)
+    plane_cot.finish()
+
+
+def split_rows(whole, split, n):
+    blk = whole.shape[1] * 2 // n
+    for zy in range(n // 2):
+        z, y = divmod(zy, 2)
+        split[y, :, z * blk : (z + 1) * blk] = whole[:, zy * blk : (zy + 1) * blk]
+
+
+class Plane:
+    def __init__(self, place, split, left, send, recv, local, tokens):
+        self.place, self.tokens, self.left = place, tokens, left
+        to = left.at[aligned(place.p, tokens), :]
+        self.own = pltpu.make_async_copy(split.at[place.y], to, local)
+        self.to_core = remote(split.at[place.y], to, send.at[0], recv.at[0], place.core)
+        self.to_side = remote(split.at[1 - place.y], to, send.at[1], recv.at[1], place.side)
+        passed = left.at[aligned(place.side_p, tokens), :]
+        self.on = remote(passed, passed, send.at[2], recv.at[2], place.core)
+
+    def start(self):
+        self.to_side.start()
+        self.own.start()
+        self.to_core.start()
+
+    def forward(self):
+        self.to_side.wait()
+        self.on.start()
+
+    def finish(self):
+        self.own.wait()
+        self.to_core.wait()
+        self.on.wait()
+
+
+def vm(shape, dtype):
+    return jax.ShapeDtypeStruct(shape, dtype)
+
+
+def forward_part(geo, x, cot, keys, values, segf, gain_one, gain_two, wq, wo):
+    n, rows, tok, width, half, heads, length = geo
+    tokens = rows * tok
+    dma = pltpu.SemaphoreType.DMA
+    anywhere, here = pl.BlockSpec(memory_space=pl.ANY), pl.BlockSpec(memory_space=pltpu.VMEM)
+    outs = [
+        vm((tokens, width), BF),
+        vm((tokens, width), BF),
+        vm((PLANE * tokens, width // 2), BF),
+        vm((tokens, width), F32),
+        vm((tokens, width), BF),
+        vm((2, tokens, width // 2), BF),
+        vm((tokens, half), BF),
+        vm((length, HEAD_DIM), BF),
+        vm((length, HEAD_DIM), BF),
+        vm((length, HEAD_DIM), BF),
+        vm((length, HEAD_DIM), BF),
+        vm((1, length), F32),
+        vm((n, 1, tok), F32),
+    ]
+    chunks = 4
+    return pl.pallas_call(
+        functools.partial(forward_kernel, geo),
+        out_shape=outs,
+        in_specs=[anywhere] * 5 + [here] * 2 + [anywhere] * 2,
+        out_specs=[here] * len(outs),
+        scratch_shapes=[
+            pltpu.VMEM(wq.shape, BF),
+            pltpu.VMEM(wo.shape, BF),
+            pltpu.VMEM((tokens, width), BF),
+            pltpu.VMEM((tokens, half), BF),
+            pltpu.VMEM((HEAD_DIM, length), BF),
+            pltpu.VMEM((1, length), F32),
+            pltpu.VMEM((length, LANE), F32),
+            pltpu.VMEM((chunks, tokens, width // chunks), BF),
+            pltpu.VMEM((chunks, tokens, width // chunks), BF),
+            pltpu.VMEM((2, tokens, width // 2), BF),
+            dma((2,)), dma((2,)), dma((5, n)), dma((5, n)), dma((chunks,)), dma((chunks,)), dma((3,)), dma((3,)), dma((10,)),
+        ],
+        compiler_params=pltpu.CompilerParams(
+            collective_id=0, has_side_effects=True, vmem_limit_bytes=48 * MIB
+        ),
+        name="attention_forward",
+    )(x, cot, keys, values, segf, gain_one, gain_two, wq, wo)
+
+
+def ffn_kernel(
+    blk, ff, x_ref, g_ref, wg_ref, wu_ref, wd_ref, hidden, d_gate, d_up, d_two, mixed, acc_two, acc_mixed
+):
+    i = pl.program_id(0)
+
+    @pl.when(i == 0)
+    def _():
+        acc_two[...] = jnp.zeros_like(acc_two)
+        acc_mixed[...] = jnp.zeros_like(acc_mixed)
+
+    inside = lax.broadcasted_iota(jnp.int32, wg_ref.shape, 1) < ff - i * blk
+    wg, wu, wd = (jnp.where(inside, w[...], jnp.zeros((), BF)) for w in (wg_ref, wu_ref, wd_ref))
+    x, g = x_ref[...], g_ref[...]
+    gate, up = dot_nn(x, wg), dot_nn(x, wu)
+    d_hid = dot_nn(g, wd)
+    sigma = jax.nn.sigmoid(gate)
+    act = gate * sigma
+    hid = (act * up).astype(BF)
+    dg = (d_hid * up * sigma * (1.0 + gate * (1.0 - sigma))).astype(BF)
+    du = (d_hid * act).astype(BF)
+    hidden[...], d_gate[...], d_up[...] = hid, dg, du
+    acc_two[...] += dot_nt(dg, wg) + dot_nt(du, wu)
+    acc_mixed[...] += dot_nt(hid, wd)
+
+    @pl.when(i == pl.num_programs(0) - 1)
+    def _():
+        d_two[...] = acc_two[...].astype(BF)
+        mixed[...] = acc_mixed[...].astype(BF)
+
+
+def ffn_part(padded, normed_two, cot_all, wg, wu, wd):
+    tokens, width = normed_two.shape
+    ff = wg.shape[1]
+    blk = 256
+    whole = pl.BlockSpec((tokens, width), lambda i: (0, 0))
+    weight = pl.BlockSpec((width, blk), lambda i: (0, i))
+    out = pl.BlockSpec((tokens, blk), lambda i: (0, i))
+    return pl.pallas_call(
+        functools.partial(ffn_kernel, blk, ff),
+        grid=(padded // blk,),
+        out_shape=[vm((tokens, padded), BF)] * 3 + [vm((tokens, width), BF)] * 2,
+        in_specs=[whole, whole, weight, weight, weight],
+        out_specs=[out, out, out, whole, whole],
+        scratch_shapes=[pltpu.VMEM((tokens, width), F32)] * 2,
+        compiler_params=pltpu.CompilerParams(
+            dimension_semantics=("arbitrary",), vmem_limit_bytes=48 * MIB
+        ),
+        name="feed_forward",
+    )(normed_two, cot_all, wg, wu, wd)
+
+
+class Gather:
+    def __init__(self, place, whole, land, send, recv, local, tokens):
+        cols = land.shape[1]
+        to = land.at[aligned(place.p, tokens), :]
+
+        def half(c):
+            return whole.at[:, aligned(c, cols)]
+
+        c = place.c
+        self.own = pltpu.make_async_copy(half(c), to, local)
+        self.away = [
+            remote(half(c), to, send.at[0], recv.at[0], place.side),
+            remote(half(1 - c), to, send.at[1], recv.at[1], place.cross),
+            remote(half(1 - c), to, send.at[2], recv.at[2], place.core),
+        ]
+
+    def start(self):
+        self.own.start()
+        for copy in self.away:
+            copy.start()
+
+    def wait(self):
+        self.own.wait()
+        for copy in self.away:
+            copy.wait()
+
+
+class Line:
+    def __init__(self, place, nz, blk, land, left, move, got, total, out, sems, work):
+        self.place, self.nz, self.blk = place, nz, blk
+        self.land, self.left, self.move, self.got, self.total, self.out = land, left, move, got, total, out
+        self.cols = land.shape[1]
+        self.mv, self.lv, self.acc, self.stage, self.load_sem = work
+        self.send, self.recv, self.end_s, self.end_r, self.end_l = sems
+
+    def load(self, left_too):
+        a = pltpu.make_async_copy(self.land, self.mv.at[:, : self.cols], self.load_sem.at[0])
+        a.start()
+        if left_too:
+            b = pltpu.make_async_copy(self.left, self.lv, self.load_sem.at[1])
+            b.start()
+            b.wait()
+        a.wait()
+
+    def product(self, b):
+        return dot_tn(self.lv[:, aligned(b, self.blk)], self.mv[:, : self.cols])
+
+    def take(self, slot):
+        self.arrival(slot).wait_recv()
+        copy = pltpu.make_async_copy(self.got.at[slot], self.stage.at[:, : self.cols], self.load_sem.at[2])
+        copy.start()
+        copy.wait()
+        return self.stage[:, : self.cols].astype(F32)
+
+    def arrival(self, slot):
+        return remote(self.move.at[0], self.got.at[slot], self.send.at[0], self.recv.at[slot], self.place.core)
+
+    def route(self, j):
+        z, nz = self.place.z, self.nz
+        b = jnp.where(z < nz // 2, nz - 1 - j, j)
+        b = jnp.where((j == nz - 2) & (z == 1), 0, b)
+        b = jnp.where((j == nz - 2) & (z == nz - 2), nz - 1, b)
+        up = b > z
+        to = jnp.where(up, z + 1, z - 1)
+        slot_in = jnp.where(up, b - z, nz - z + b)
+        slot_out = jnp.where(up, b - to, nz - to + b)
+        keep = jnp.where(up, b - 1, b)
+        last = jnp.where(up, z == 0, z == nz - 1)
+        device = (to * PLANE + self.place.p, self.place.t)
+        out = remote(self.move.at[keep], self.got.at[slot_out], self.send.at[keep], self.recv.at[slot_out], device)
+        return b, slot_in, keep, last, out
+
+    def step(self, j):
+        b, slot_in, keep, last, out = self.route(j)
+        self.acc[:, : self.cols] = self.product(b)
+
+        @pl.when(last)
+        def _():
+            self.move[keep] = self.acc[:, : self.cols].astype(BF)
+
+        @pl.when(jnp.logical_not(last))
+        def _():
+            self.move[keep] = (self.acc[:, : self.cols] + self.take(slot_in)).astype(BF)
+
+        out.start()
+
+    def steps(self):
+        def one(j, unused):
+            self.step(j)
+            return unused
+
+        lax.fori_loop(0, self.nz - 1, one, 0)
+
+    def own_block(self):
+        self.total[...] = self.product(self.place.z)
+
+    def ends(self):
+        half = self.blk // 2
+        c, core = self.place.c, self.place.core
+        columns = self.out.at[:, aligned(c, self.cols)]
+        away = remote(self.total.at[aligned(1 - c, half), :], columns, self.end_s, self.end_r, core)
+        here = pltpu.make_async_copy(self.total.at[aligned(c, half), :], columns, self.end_l)
+        return away, here
+
+    def finish(self):
+        z, nz = self.place.z, self.nz
+
+        @pl.when(z > 0)
+        def _():
+            self.total[...] += self.take(0)
+
+        @pl.when(z < nz - 1)
+        def _():
+            self.total[...] += self.take(nz)
+
+        for copy in self.ends():
+            copy.start()
+
+    def drain(self):
+        def one(j, unused):
+            self.route(j)[4].wait_send()
+            return unused
+
+        lax.fori_loop(0, self.nz - 1, one, 0)
+        for copy in self.ends():
+            copy.wait()
+
+
+def backward_kernel(
+    geo,
+    hidden, d_gate, d_up, d_two, mixed, left_cot, left_two, middle_in, x_in, cot_in, att_in,
+    q_in, k_in, v_in, o_in, lse_in, seg_in, wo_in, wq_in, gain_one, gain_two,
+    ffn_in, input_grad, d_keys, d_values, gains,
+    out_down, out_gate, out_up, out_out, out_query,
+    m_down, m_gate, m_up, m_out, m_query, l_two, l_err, l_one,
+    g_down, g_gate, g_up, g_out, g_query,
+    mid, x_all, cot_all, two_own, two_in, one_part, one_in, err, one, weight, d_att,
+    uq, uk, uv, uo, udo, lse, seg_all, seg_row, seg_col, k_t, delta, dk_acc, dv_acc, udq, udk, udv, dq,
+    gain_part, gain_in,
+    s_down, s_gate, s_up, s_out, s_query, t_down, t_gate, t_up, t_out, t_query,
+    mv, lv, acc, stage,
+    tp_s, tp_r, a_s, a_r, me_s, me_r, le_s, le_r, c_s, c_r, e_s, e_r, e_l, loc, work_sem,
+):
+    n, rows, tok, width, half, heads, length = geo
+    tokens = rows * tok
+    blk = 2 * width // n
+    nz = n // PLANE
+    place = Place(n)
+    s, t, z = place.s, place.t, place.z
+    row_s, head_s = s // heads, lax.rem(s, heads)
+    place.enter()
+    mine = aligned(t, half)
+    chunk = tokens // 4
+
+    def two_copy(i):
+        at = aligned(i, chunk)
+        return remote(d_two.at[at, :], two_in.at[at, :], tp_s.at[i], tp_r.at[i], place.twin)
+
+    for i in range(4):
+        two_copy(i).start()
+    ffn_copy = remote(mixed.at[:, aligned(1 - t, half)], ffn_in, tp_s.at[4], tp_r.at[4], place.twin)
+    ffn_copy.start()
+
+    gathers = [
+        Gather(place, whole, land, me_s.at[i], me_r.at[i], loc.at[i], tokens)
+        for i, (whole, land) in enumerate(
+            ((hidden, m_down), (d_gate, m_gate), (d_up, m_up), (att_in, m_out), (dq, m_query))
+        )
+    ]
+    lefts = [
+        Plane(place, split, land, le_s.at[i], le_r.at[i], loc.at[5 + i], tokens)
+        for i, (split, land) in enumerate(((left_two, l_two), (err, l_err), (one, l_one)))
+    ]
+    work = (mv, lv, acc, stage, work_sem)
+    lines = [
+        Line(place, nz, blk, *refs, (c_s.at[i], c_r.at[i], e_s.at[i], e_r.at[i], e_l.at[i]), work)
+        for i, refs in enumerate((
+            (m_down, left_cot, s_down, g_down, t_down, out_down),
+            (m_gate, l_two, s_gate, g_gate, t_gate, out_gate),
+            (m_up, l_two, s_up, g_up, t_up, out_up),
+            (m_out, l_err, s_out, g_out, t_out, out_out),
+            (m_query, l_one, s_query, g_query, t_query, out_query),
+        ))
+    ]
+    down, gate, up, out, query = lines
+    gathers[0].start()
+
+    loads = [
+        pltpu.make_async_copy(a, b, loc.at[8 + i])
+        for i, (a, b) in enumerate((
+            (middle_in, mid), (d_two, two_own), (cot_in, cot_all), (wo_in, weight), (x_in, x_all),
+            (q_in, uq), (k_in, uk), (v_in, uv), (o_in, uo), (lse_in, lse), (seg_in, seg_all),
+        ))
+    ]
+    for copy in loads:
+        copy.start()
+    for copy in loads[:4]:
+        copy.wait()
+
+    spread_att = Spread(
+        place,
+        lambda d: d_att.at[aligned(d // heads, tok), aligned(lax.rem(d, heads), HEAD_DIM)],
+        lambda: udo.at[aligned(s, tok), :],
+        a_s.at[0], a_r.at[0], loc.at[19],
+    )
+    fine = 32
+
+    def second_norm(i, gain_sum):
+        two_copy(i).wait()
+
+        def some(j, gain_sum):
+            at = aligned(i * (chunk // fine) + j, fine)
+            m = mid[at, :]
+            d2 = two_own[at, :].astype(F32) + two_in[at, :].astype(F32)
+            root = lax.rsqrt(jnp.mean(m * m, axis=-1, keepdims=True) + EPSILON)
+            gained = d2 * gain_two[...]
+            scaled = m * root
+            gain_sum = gain_sum + jnp.sum(d2 * scaled, axis=0, keepdims=True)
+            slope = jnp.mean(gained * scaled, axis=-1, keepdims=True)
+            dm = cot_all[at, :].astype(F32) + root * (gained - scaled * slope)
+            mid[at, :] = dm
+            low = dm.astype(BF)
+            for zy in range(n // 2):
+                zz, yy = divmod(zy, 2)
+                err[yy, at, zz * blk : (zz + 1) * blk] = low[:, zy * blk : (zy + 1) * blk]
+            return gain_sum
+
+        gain_sum = lax.fori_loop(0, chunk // fine, some, gain_sum)
+        at = aligned(i, chunk)
+        total = jnp.zeros((chunk, half), F32)
+        for zy in range(n // 2):
+            zz, yy = divmod(zy, 2)
+            total += dot_nn(err[yy, at, zz * blk : (zz + 1) * blk], weight[zy * blk : (zy + 1) * blk, :])
+        d_att[at, :] = total.astype(BF)
+        return gain_sum
+
+    gain_sum = jnp.zeros((1, width), F32)
+    per_row = tok // chunk
+    for r in range(rows):
+        gain_sum = lax.fori_loop(r * per_row, (r + 1) * per_row, second_norm, gain_sum)
+        lax.fori_loop(r * heads, (r + 1) * heads, spread_att.start_to, 0)
+    for i in range(n):
+        gain_part[0, i] = gain_sum[:, i * (width // n) : (i + 1) * (width // n)]
+    spread_gain = [
+        Spread(place, lambda d, g=g: gain_part.at[g, d], lambda g=g: gain_in.at[g, s], a_s.at[4 + g], a_r.at[4 + g], loc.at[23 + g])
+        for g in range(2)
+    ]
+    spread_gain[0].start()
+    load_q = pltpu.make_async_copy(wq_in, weight, loc.at[25])
+    load_q.start()
+
+    lefts[0].start()
+    gathers[1].start()
+    gathers[2].start()
+    lefts[1].start()
+    gathers[3].start()
+
+    loads[4].wait()
+
+    def first_norm(j, unused):
+        at = aligned(j, fine)
+        x = x_all[at, :].astype(F32)
+        root = lax.rsqrt(jnp.mean(x * x, axis=-1, keepdims=True) + EPSILON)
+        low = (x * root * gain_one[...]).astype(BF)
+        for zy in range(n // 2):
+            zz, yy = divmod(zy, 2)
+            one[yy, at, zz * blk : (zz + 1) * blk] = low[:, zy * blk : (zy + 1) * blk]
+        return unused
+
+    lax.fori_loop(0, tokens // fine, first_norm, 0)
+
+    for copy in loads[5:]:
+        copy.wait()
+    attention_masks(seg_all, seg_row, seg_col, n, tok)
+
+    def turn(i, unused):
+        at = aligned(i, tok)
+        k_t[:, at] = jnp.transpose(uk[at, :].astype(F32)).astype(BF)
+        return unused
+
+    lax.fori_loop(0, n, turn, 0)
+    dk_acc[...] = jnp.zeros_like(dk_acc)
+    dv_acc[...] = jnp.zeros_like(dv_acc)
+
+    gathers[0].wait()
+    down.load(True)
+    at_end = (z == 0) | (z == nz - 1)
+
+    @pl.when(at_end)
+    def _():
+        down.steps()
+
+    spread_att.wait()
+
+    def turn_delta(i, unused):
+        at = aligned(i, tok)
+        both = udo[at, :].astype(F32) * uo[at, :].astype(F32)
+        delta[:, at] = jnp.sum(jnp.transpose(both), axis=0, keepdims=True)
+        return unused
+
+    lax.fori_loop(0, n, turn_delta, 0)
+
+    block = 512
+    owners = block // tok
+
+    def home(ref):
+        return lambda: ref.at[aligned(row_s, tok), aligned(head_s, HEAD_DIM)]
+
+    spread_dq, spread_dk, spread_dv = (
+        Spread(place, lambda d, unit=unit: unit.at[aligned(d, tok), :], home(whole), a_s.at[i], a_r.at[i], loc.at[19 + i])
+        for i, unit, whole in ((1, udq, dq), (2, udk, d_keys), (3, udv, d_values))
+    )
+
+    def query_step(i, unused):
+        qi = length // block - 1 - i
+        qat = aligned(qi, block)
+        qb, dob = uq[qat, :], udo[qat, :]
+
+        def key_step(kj, dq_t):
+            kat = aligned(kj, block)
+            scores = dot_nt(uk[kat, :], qb) - lse[:, qat]
+            probs = jnp.exp(jnp.where(readable(seg_col, seg_row, kj, qi, block), scores, NEGATIVE_FILL))
+            d_probs = dot_nt(uv[kat, :], dob)
+            d_scores = (probs * (d_probs - delta[:, qat])).astype(BF)
+            dv_acc[kat, :] += dot_nn(probs.astype(BF), dob)
+            dk_acc[kat, :] += dot_nn(d_scores, qb)
+            return dq_t + dot_nn(k_t[:, kat], d_scores)
+
+        dq_t = lax.fori_loop(0, qi + 1, key_step, jnp.zeros((HEAD_DIM, block), F32))
+        udq[qat, :] = jnp.transpose(dq_t).astype(BF)
+        lax.fori_loop(qi * owners, (qi + 1) * owners, spread_dq.start_to, 0)
+        udk[qat, :] = dk_acc[qat, :].astype(BF)
+        udv[qat, :] = dv_acc[qat, :].astype(BF)
+        lax.fori_loop(qi * owners, (qi + 1) * owners, spread_dk.start_to, 0)
+        lax.fori_loop(qi * owners, (qi + 1) * owners, spread_dv.start_to, 0)
+        return unused
+
+    lax.fori_loop(0, length // block, query_step, 0)
+
+    @pl.when(jnp.logical_not(at_end))
+    def _():
+        down.steps()
+
+    down.own_block()
+    lefts[0].forward()
+    gathers[1].wait()
+    lefts[0].finish()
+    gate.load(True)
+    gate.steps()
+    gate.own_block()
+
+    load_q.wait()
+    spread_dq.wait()
+    gathers[4].start()
+    lefts[2].start()
+
+    def one_copy(i):
+        at = aligned(i, chunk)
+        return remote(one_part.at[at, :], one_in.at[at, :], tp_s.at[5 + i], tp_r.at[5 + i], place.twin)
+
+    def back_query(i, unused):
+        at = aligned(i, chunk)
+        one_part[at, :] = (dot_nt(dq[at, :], weight[...]) * HEAD_DIM ** (-0.5)).astype(BF)
+        one_copy(i).start()
+        return unused
+
+    lax.fori_loop(0, 4, back_query, 0)
+
+    gathers[2].wait()
+    up.load(False)
+    up.steps()
+    up.own_block()
+    down.finish()
+
+    lefts[1].forward()
+
+    def last_norm(i, gain_sum):
+        one_copy(i).wait()
+
+        def some(j, gain_sum):
+            at = aligned(i * (chunk // fine) + j, fine)
+            x = x_all[at, :].astype(F32)
+            d1 = one_part[at, :].astype(F32) + one_in[at, :].astype(F32)
+            root = lax.rsqrt(jnp.mean(x * x, axis=-1, keepdims=True) + EPSILON)
+            gained = d1 * gain_one[...]
+            scaled = x * root
+            gain_sum = gain_sum + jnp.sum(d1 * scaled, axis=0, keepdims=True)
+            slope = jnp.mean(gained * scaled, axis=-1, keepdims=True)
+            mid[at, :] = mid[at, :] + root * (gained - scaled * slope)
+            return gain_sum
+
+        return lax.fori_loop(0, chunk // fine, some, gain_sum)
+
+    gain_sum = lax.fori_loop(0, 4, last_norm, jnp.zeros((1, width), F32))
+    for i in range(n):
+        gain_part[1, i] = gain_sum[:, i * (width // n) : (i + 1) * (width // n)]
+    spread_gain[1].start()
+    give = pltpu.make_async_copy(mid.at[:, mine], input_grad, loc.at[26])
+    give.start()
+
+    gathers[3].wait()
+    lefts[1].finish()
+    out.load(True)
+    out.steps()
+    out.own_block()
+    gate.finish()
+
+    lefts[2].forward()
+    gathers[4].wait()
+    lefts[2].finish()
+    query.load(True)
+    query.steps()
+    query.own_block()
+    up.finish()
+    out.finish()
+    query.finish()
+
+    spread_dk.wait()
+    spread_dv.wait()
+    for g in range(2):
+        spread_gain[g].wait()
+        gains[g] = jnp.sum(gain_in[g], axis=0)
+    ffn_copy.wait()
+    give.wait()
+    for line in lines:
+        line.drain()
+
+
+def backward_part(geo, ffn, forward, wo, wq, gain_one, gain_two):
+    n, rows, tok, width, half, heads, length = geo
+    tokens = rows * tok
+    blk = 2 * width // n
+    nz = n // PLANE
+    hidden, d_gate, d_up, d_two, mixed = ffn
+    x_all, cot_all, left_cot, middle, _, left_two, attended, uq, uk, uv, uo, lse, seg_all = forward
+    dma = pltpu.SemaphoreType.DMA
+    anywhere, here = pl.BlockSpec(memory_space=pl.ANY), pl.BlockSpec(memory_space=pltpu.VMEM)
+    wide = (hidden.shape[1] // 2,) * 3 + (half // 2,) * 2
+    outs = [
+        (vm((tokens, half), BF), anywhere),
+        (vm((tokens, half), F32), anywhere),
+        (vm((tokens, half), BF), anywhere),
+        (vm((tokens, half), BF), anywhere),
+        (vm((2, 1, width // n), F32), here),
+        *((vm((blk // 2, 2 * cols), F32), anywhere) for cols in wide),
+        *((vm((PLANE * tokens, cols), BF), anywhere) for cols in wide),
+        *((vm((PLANE * tokens, width // 2), BF), anywhere) for _ in range(3)),
+        *((vm((nz + 1, blk, cols), BF), anywhere) for cols in wide),
+    ]
+    inputs = [
+        hidden, d_gate, d_up, d_two, mixed, left_cot, left_two, middle, x_all, cot_all, attended,
+        uq, uk, uv, uo, lse, seg_all, wo, wq, gain_one, gain_two,
+    ]
+    big = max(wide)
+    unit = pltpu.VMEM((length, HEAD_DIM), BF)
+    unit_sum = pltpu.VMEM((length, HEAD_DIM), F32)
+    line = pltpu.VMEM((1, length), F32)
+    act = pltpu.VMEM((tokens, width), BF)
+    split = pltpu.VMEM((2, tokens, width // 2), BF)
+    scratch = [
+        pltpu.VMEM((tokens, width), F32), act, act, act, act, act, act, split, split,
+        pltpu.VMEM(wo.shape, BF), pltpu.VMEM((tokens, half), BF),
+        unit, unit, unit, unit, unit, line, pltpu.VMEM((n, 1, tok), F32), line,
+        pltpu.VMEM((length, LANE), F32), pltpu.VMEM((HEAD_DIM, length), BF), line,
+        unit_sum, unit_sum, unit, unit, unit, pltpu.VMEM((tokens, half), BF),
+        pltpu.VMEM((2, n, 1, width // n), F32), pltpu.VMEM((2, n, 1, width // n), F32),
+        *(pltpu.VMEM((nz - 1, blk, cols), BF) for cols in wide),
+        *(pltpu.VMEM((blk, cols), F32) for cols in wide),
+        pltpu.VMEM((PLANE * tokens, big), BF), pltpu.VMEM((PLANE * tokens, width // 2), BF),
+        pltpu.VMEM((blk, big), F32), pltpu.VMEM((blk, big), BF),
+        dma((9,)), dma((9,)), dma((6, n)), dma((6, n)), dma((5, 3)), dma((5, 3)), dma((3, 3)), dma((3, 3)),
+        dma((5, nz - 1)), dma((5, nz + 1)), dma((5,)), dma((5,)), dma((5,)), dma((27,)), dma((3,)),
+    ]
+    return pl.pallas_call(
+        functools.partial(backward_kernel, geo),
+        out_shape=[o for o, _ in outs],
+        in_specs=[anywhere] * (len(inputs) - 2) + [here] * 2,
+        out_specs=[spec for _, spec in outs],
+        scratch_shapes=scratch,
+        compiler_params=pltpu.CompilerParams(
+            collective_id=1, has_side_effects=True, vmem_limit_bytes=62 * MIB
+        ),
+        name="backward",
+    )(*inputs)
+
+
+def fast_device(
+    n, inputs, segments, keys, values, attn_gain, query_weight, out_weight, ffn_gain, gate_weight, up_weight, down_weight,
+    cotangent,
+):
+    rows, tok, half = inputs.shape
+    tokens, width, ff = rows * tok, query_weight.shape[0], gate_weight.shape[1]
+    heads = half // HEAD_DIM
+    geo = (n, rows, tok, width, half, heads, n * tok)
+    padded = -(-ff // (2 * LANE)) * 2 * LANE
+
+    def flat(a):
+        return a.reshape(tokens, half)
+
+    segf = segments.astype(F32).reshape(rows, 1, tok)
+    gain_one, gain_two = attn_gain.reshape(1, width), ffn_gain.reshape(1, width)
+    forward = forward_part(
+        geo, flat(inputs), flat(cotangent), flat(keys), flat(values), segf, gain_one, gain_two, query_weight, out_weight
+    )
+    x_all, cot_all, _, middle, normed_two = forward[:5]
+    ffn = ffn_part(padded, normed_two, cot_all, gate_weight, up_weight, down_weight)
+    back = backward_part(geo, ffn, forward, out_weight, query_weight, gain_one, gain_two)
+    ffn_in, input_grad, d_keys, d_values, gains, g_down, g_gate, g_up, g_out, g_query = back[:10]
+    at = lax.axis_index("tp") * half
+    mixed = (
+        lax.dynamic_slice_in_dim(middle, at, half, 1)
+        + lax.dynamic_slice_in_dim(ffn[4], at, half, 1).astype(F32)
+        + ffn_in.astype(F32)
+    ).astype(BF)
+
+    def shaped(a):
+        return a.reshape(rows, tok, half)
+
+    return (
+        shaped(mixed),
+        shaped(input_grad),
+        shaped(d_keys.astype(F32)),
+        shaped(d_values.astype(F32)),
+        gains[1, 0],
+        g_query * HEAD_DIM ** (-0.5),
+        g_out,
+        gains[0, 0],
+        g_gate[:, :ff],
+        g_up[:, :ff],
+        g_down[:, :ff],
+    )
 
 
 def inverse_root(stream):
@@ -302,6 +1243,15 @@
         P("seq", "tp"),
         P("seq", "tp"),
     )
+    n = mesh.shape["seq"]
+
+    def step(inputs, *others):
+        rows, tok, half = inputs.shape
+        units = rows * (half // HEAD_DIM)
+        if units == n == PLANE * PLANE and 4 * tok == 512 and mesh.shape["tp"] == 2:
+            return fast_device(n, inputs, *others)
+        return per_device(inputs, *others)
+
     return jax.shard_map(
-        per_device, mesh=mesh, in_specs=in_specs, out_specs=out_specs, check_vma=False
-    )
+        step, mesh=mesh, in_specs=in_specs, out_specs=out_specs, check_vma=False
+    )

time: 1830 us -> 457 us (0.25)
  waiting for transfers between devices: 1410 us -> 0 us
  Pallas kernels: 0 us -> 377 us
  matrix products: 113 us -> 0 us
  blocking collectives: 110 us -> 0 us
  local copies, waits for them, and re-layouts: 130 us -> 68.9 us
  other arithmetic: 33.4 us -> 8.12 us
    reduce_scatter x8 -> x0, waiting for transfers between devices: 1180 us -> none  [the longest x3 679 us: per_device(): lax.psum_scatter((gate_term, up_term, down_term, gain_term), 'seq', scatt...]
    pallas_call x0 -> x3, Pallas kernels: none -> 377 us  [the longest x1 266 us: backward_part(): pl.pallas_call(functools.partial(backward_kernel, geo), out_shape=[o for...]
    all_gather x4 -> x0, waiting for transfers between devices: 143 us -> none  [the longest x1 79 us: per_device(): value_piece = lax.all_gather(values, 'seq', axis=1, tiled=True)]
    dot_general x22 -> x0, matrix products: 113 us -> none  [the longest x1 13.4 us: per_device(): jnp.einsum('rtd,df->rtf', normed_two, gate_weight, preferred_element_type...]
    psum x3 -> x0, waiting for transfers between devices: 85.5 us -> none  [the longest x1 44.6 us: per_device(): lax.psum(branch.astype(jnp.bfloat16), 'tp').astype(jnp.float32)]
    dynamic_update_slice x12 -> x0, local copies, waits for them, and re-layouts: 76.9 us -> none  [the longest x8 55.3 us: back_step(): lax.dynamic_update_slice_in_dim(value_terms, value_part, begin, 1)]
    unnamed x1 -> x0, blocking collectives: 74.8 us -> none
    unnamed x67 -> x62, local copies, waits for them, and re-layouts: 15.1 us -> 68.4 us
  transfers between devices with their start and end apart: 15 -> 0, of which waited for: 13 -> 0; matrix products, arithmetic and copies ran while one was open for 13% -> 0% of each run, Pallas kernels for 0% -> 0%
where the time goes in v1:
time: 457 us; the launch traced here: 455 us
  Pallas kernels  377 us (82%)
  local copies, waits for them, and re-layouts  68.9 us (15%)
  other arithmetic  8.12 us (2%)
    pallas_call x1, Pallas kernels, backward_part(): pl.pallas_call(functools.partial(backward_kernel, geo), out_shape=[o for...  266 us
    pallas_call x1, Pallas kernels, forward_part(): pl.pallas_call(functools.partial(forward_kernel, geo), out_shape=outs, in...  80.3 us
    unnamed x62, local copies, waits for them, and re-layouts  68.4 us
    pallas_call x1, Pallas kernels, ffn_part(): pl.pallas_call(functools.partial(ffn_kernel, blk, ff), grid=(padded // bl...  30.4 us

profile of v1, /device:TPU:0, one launch (start us, length us, event | category | flops | bytes accessed | tf_op | source)
XLA Modules:
  0.0 454.9 jit_solution(4645736098714637312)
XLA Ops:
  0.6 0.7 convert_element_type.14
  1.3 0.0 copy-start.12
  1.3 1.0 copy-done.12
  2.4 1.0 copy-done.13
  3.4 1.0 copy-done.14
  4.5 1.0 copy-done.15
  5.5 0.7 copy-done.16
  6.2 0.7 copy-done.17
  6.9 80.3 %attention_forward.1 = (bf16[256,2048]{1,0:T(8,128)(2,1)S(1)}, bf16[256,2048]{1,0:T(8,128)(2,1)}, bf16[1024,1024]{1,0:T(8,128)(2,1)}, f32[256,2048]{1,0:T(8,128)...) custom-call(bf16[256,1024]{1,0:T(8,128)(2,1)S(1)} %bitcast.20, ...), custom_call_target="tpu_custom_call" | custom-call | tf_op jit(solution)/shard_map/attention_forward/pallas_call | solution.py:348
  87.2 0.0 copy-start.4
  87.2 1.0 copy-done.4
  88.2 0.8 copy-done.7
  89.0 0.8 copy-done.8
  89.7 0.8 copy-done.9
  90.5 0.8 copy-done.10
  91.3 0.8 copy-done.11
  92.1 0.6 copy-done.18
  92.7 0.6 copy-done.19
  93.3 15.3 %copy.23.wg_ref = bf16[2048,2752]{1,0:T(8,128)(2,1)} copy(bf16[2048,2752]{0,1:T(8,128)(2,1)} %param.20) | data formatting | bytes 22544384 | tf_op args[8]
  108.6 15.3 %copy.24.wu_ref = bf16[2048,2752]{1,0:T(8,128)(2,1)} copy(bf16[2048,2752]{0,1:T(8,128)(2,1)} %param.21) | data formatting | bytes 22544384 | tf_op args[9]
  123.9 15.3 %copy.25.wd_ref = bf16[2048,2752]{1,0:T(8,128)(2,1)} copy(bf16[2048,2752]{0,1:T(8,128)(2,1)} %param.22) | data formatting | bytes 22544384 | tf_op args[10]
  139.1 0.0 copy-done
  139.1 0.0 copy-done.6
  139.1 30.4 %feed_forward.1 = (bf16[256,2816]{1,0:T(8,128)(2,1)S(1)}, bf16[256,2816]{1,0:T(8,128)(2,1)}, bf16[256,2816]{1,0:T(8,128)(2,1)}, bf16[256,2048]{1,0:T(8,128)(2,1)S(1)}, bf16[256,2048]{1,0:T(8,128)(2,1)S(1)}) custom-call(bf16[256,2048]{1,0:T(8,128)(2,1)S(1)} %copy-done.6, bf16[256,2048]{1,0:T(8,128)(2,1)S(1)} %copy-done, bf16[2048,2752]{1,0:T(8,128)(2,1)} %copy.23.wg_ref, ...), custom_call_target="tpu_custom_call" | custom-call | tf_op jit(solution)/shard_map/feed_forward/pallas_call | solution.py:410
  169.6 1.0 copy-done.1
  170.6 1.1 copy-done.3
  171.7 1.0 copy-done.5
  172.6 266.4 %backward.1 = (bf16[256,1024]{1,0:T(8,128)(2,1)}, f32[256,1024]{1,0:T(8,128)}, bf16[256,1024]{1,0:T(8,128)(2,1)}, bf16[256,1024]{1,0:T(8,128)(2,1)}, f32[2,1,128...) custom-call(bf16[256,2816]{1,0:T(8,128)(2,1)} %copy-done.3, ...), custom_call_target="tpu_custom_call" | custom-call | tf_op jit(solution)/shard_map/backward/pallas_call | solution.py:897
  439.1 0.0 copy-start.22
  439.1 3.0 copy.26
  442.1 0.0 copy-done.22
  442.1 1.5 copy.27
  443.6 0.0 copy-done.21
  443.6 1.5 copy.28
  445.2 2.3 convert.2
  447.4 2.1 convert.3
  449.6 0.0 copy-done.2
  449.6 0.0 copy-done.20
  449.6 0.0 copy-start.23
  449.6 2.2 add_convert_fusion
  451.8 0.0 copy-done.25
  451.8 0.8 broadcast_multiply_fusion
  452.6 0.0 copy-done.26
  452.6 0.5 slice_bitcast_fusion
  453.1 0.0 copy-done.23
  453.1 1.0 copy.31
  454.1 0.0 copy-done.24
  454.1 0.8 copy.32
  (23 shorter events, 0.0 us)
Async XLA Ops:
  1.3 1.0 copy-start.12
  2.4 1.0 copy-start.13
  3.4 1.0 copy-start.14
  4.5 1.0 copy-start.15
  5.5 0.7 copy-start.16
  6.2 0.7 copy-start.17
  87.2 1.0 copy-start.4
  88.2 0.8 copy-start.7
  89.0 0.8 copy-start.8
  89.7 0.8 copy-start.9
  90.5 0.8 copy-start.10
  91.3 0.8 copy-start.11
  92.1 0.6 copy-start.18
  92.7 0.6 copy-start.19
  123.9 15.3 %copy-start = (bf16[256,2048]{1,0:T(8,128)(2,1)S(1)}, bf16[256,2048]{1,0:T(8,128)(2,1)}, u32[]{:S(2)}) copy-start(bf16[256,2048]{1,0:T(8,128)(2,1)} %get-tuple-element.41.g_ref.cot_in) | copy-start | bytes 3145732
  123.9 15.3 %copy-start.6 = (bf16[256,2048]{1,0:T(8,128)(2,1)S(1)}, bf16[256,2048]{1,0:T(8,128)(2,1)}, u32[]{:S(2)}) copy-start(bf16[256,2048]{1,0:T(8,128)(2,1)} %get-tuple-element.40.x_ref) | copy-start | bytes 3145732
  169.6 1.0 copy-start.1
  170.6 1.1 copy-start.3
  171.7 1.0 copy-start.5
  439.1 3.0 copy-start.22
  442.1 1.5 copy-start.21
  445.1 4.4 copy-start.2
  445.2 4.4 copy-start.20
  449.6 3.1 copy-start.26
  449.6 2.2 copy-start.25
  449.6 3.6 copy-start.23
  451.8 2.3 copy-start.24

commit v2 on v1

--- a/solution.py
+++ b/solution.py
@@ -18,7 +18,7 @@
 MESH = pl.DeviceIdType.MESH
 BF = jnp.bfloat16
 F32 = jnp.float32
-MIB = 1 << 20
+VMEM_GRANT = 62 << 20
 PLANE = 4
 LANE = 128
 
@@ -144,9 +144,10 @@
 def forward_kernel(
     geo,
     x_in, cot_in, key_in, value_in, seg_in, gain_one, gain_two, wq_in, wo_in,
+    x_out, cot_out, left_out, middle_out, two_out, split_out, att_out, q_out, k_out, v_out, o_out, lse_out, seg_out,
     x_all, cot_all, left_cot, middle, normed_two, left_two, attended, unit_q, unit_k, unit_v, unit_o, lse, seg_all,
     wq, wo, normed_one, query, value_t, seg_row, seg_col, part, part_in, cot_split,
-    tp_s, tp_r, a_s, a_r, br_s, br_r, l_s, l_r, loc,
+    tp_s, tp_r, a_s, a_r, br_s, br_r, l_s, l_r, loc, away,
 ):
     n, rows, tok, width, half, heads, length = geo
     place = Place(n)
@@ -154,6 +155,14 @@
     place.enter()
     row_s, head_s = s // heads, lax.rem(s, heads)
     half_at = aligned(t, half)
+    leaving = []
+
+    def leave(*pairs):
+        for here, there in pairs:
+            copy = pltpu.make_async_copy(here, there, away.at[len(leaving)])
+            copy.start()
+            leaving.append(copy)
+
 
     to_x = remote(x_in, x_all.at[:, half_at], tp_s.at[0], tp_r.at[0], place.twin)
     to_x.start()
@@ -191,6 +200,7 @@
         return unused
 
     lax.fori_loop(0, rows * tok // step, norm_one, 0)
+    leave((x_all, x_out))
     load_q.wait()
     query[...] = (dot_nn(normed_one[...], wq[...]) * HEAD_DIM ** (-0.5)).astype(BF)
     qrys.start()
@@ -207,6 +217,7 @@
 
     lax.fori_loop(0, n, turn, 0)
     qrys.wait()
+    leave((unit_q, q_out), (unit_k, k_out), (unit_v, v_out), (seg_all, seg_out))
 
     back = Spread(
         place,
@@ -245,6 +256,7 @@
 
     lax.fori_loop(0, length // block, query_step, 0)
 
+    leave((unit_o, o_out), (lse, lse_out))
     own_cot.wait()
     to_cot.wait()
     split_rows(cot_all, cot_split, n)
@@ -252,6 +264,7 @@
     plane_cot.start()
     load_o.wait()
     back.wait()
+    leave((attended, att_out), (cot_all, cot_out))
 
     chunks = part.shape[0]
     wide = width // chunks
@@ -283,9 +296,14 @@
         normed_two[:, at] = (middle[:, at] * root_two * gain_two[:, at]).astype(BF)
         return unused
 
+    leave((middle, middle_out))
     lax.fori_loop(0, chunks, norm_two, 0)
+    leave((normed_two, two_out))
     split_rows(normed_two, left_two, n)
     plane_cot.finish()
+    leave((left_two, split_out), (left_cot, left_out))
+    for copy in leaving:
+        copy.wait()
 
 
 def split_rows(whole, split, n):
@@ -349,8 +367,9 @@
         functools.partial(forward_kernel, geo),
         out_shape=outs,
         in_specs=[anywhere] * 5 + [here] * 2 + [anywhere] * 2,
-        out_specs=[here] * len(outs),
+        out_specs=[anywhere] * len(outs),
         scratch_shapes=[
+            *(pltpu.VMEM(o.shape, o.dtype) for o in outs),
             pltpu.VMEM(wq.shape, BF),
             pltpu.VMEM(wo.shape, BF),
             pltpu.VMEM((tokens, width), BF),
@@ -361,73 +380,22 @@
             pltpu.VMEM((chunks, tokens, width // chunks), BF),
             pltpu.VMEM((chunks, tokens, width // chunks), BF),
             pltpu.VMEM((2, tokens, width // 2), BF),
-            dma((2,)), dma((2,)), dma((5, n)), dma((5, n)), dma((chunks,)), dma((chunks,)), dma((3,)), dma((3,)), dma((10,)),
+            dma((2,)), dma((2,)), dma((5, n)), dma((5, n)), dma((chunks,)), dma((chunks,)), dma((3,)), dma((3,)), dma((10,)), dma((len(outs),)),
         ],
         compiler_params=pltpu.CompilerParams(
-            collective_id=0, has_side_effects=True, vmem_limit_bytes=48 * MIB
+            collective_id=0, has_side_effects=True, vmem_limit_bytes=VMEM_GRANT
         ),
         name="attention_forward",
     )(x, cot, keys, values, segf, gain_one, gain_two, wq, wo)
 
 
-def ffn_kernel(
-    blk, ff, x_ref, g_ref, wg_ref, wu_ref, wd_ref, hidden, d_gate, d_up, d_two, mixed, acc_two, acc_mixed
-):
-    i = pl.program_id(0)
-
-    @pl.when(i == 0)
-    def _():
-        acc_two[...] = jnp.zeros_like(acc_two)
-        acc_mixed[...] = jnp.zeros_like(acc_mixed)
-
-    inside = lax.broadcasted_iota(jnp.int32, wg_ref.shape, 1) < ff - i * blk
-    wg, wu, wd = (jnp.where(inside, w[...], jnp.zeros((), BF)) for w in (wg_ref, wu_ref, wd_ref))
-    x, g = x_ref[...], g_ref[...]
-    gate, up = dot_nn(x, wg), dot_nn(x, wu)
-    d_hid = dot_nn(g, wd)
-    sigma = jax.nn.sigmoid(gate)
-    act = gate * sigma
-    hid = (act * up).astype(BF)
-    dg = (d_hid * up * sigma * (1.0 + gate * (1.0 - sigma))).astype(BF)
-    du = (d_hid * act).astype(BF)
-    hidden[...], d_gate[...], d_up[...] = hid, dg, du
-    acc_two[...] += dot_nt(dg, wg) + dot_nt(du, wu)
-    acc_mixed[...] += dot_nt(hid, wd)
-
-    @pl.when(i == pl.num_programs(0) - 1)
-    def _():
-        d_two[...] = acc_two[...].astype(BF)
-        mixed[...] = acc_mixed[...].astype(BF)
-
-
-def ffn_part(padded, normed_two, cot_all, wg, wu, wd):
-    tokens, width = normed_two.shape
-    ff = wg.shape[1]
-    blk = 256
-    whole = pl.BlockSpec((tokens, width), lambda i: (0, 0))
-    weight = pl.BlockSpec((width, blk), lambda i: (0, i))
-    out = pl.BlockSpec((tokens, blk), lambda i: (0, i))
-    return pl.pallas_call(
-        functools.partial(ffn_kernel, blk, ff),
-        grid=(padded // blk,),
-        out_shape=[vm((tokens, padded), BF)] * 3 + [vm((tokens, width), BF)] * 2,
-        in_specs=[whole, whole, weight, weight, weight],
-        out_specs=[out, out, out, whole, whole],
-        scratch_shapes=[pltpu.VMEM((tokens, width), F32)] * 2,
-        compiler_params=pltpu.CompilerParams(
-            dimension_semantics=("arbitrary",), vmem_limit_bytes=48 * MIB
-        ),
-        name="feed_forward",
-    )(normed_two, cot_all, wg, wu, wd)
-
-
 class Gather:
-    def __init__(self, place, whole, land, send, recv, local, tokens):
+    def __init__(self, place, whole, stride, first, land, send, recv, local, tokens):
         cols = land.shape[1]
         to = land.at[aligned(place.p, tokens), :]
 
         def half(c):
-            return whole.at[:, aligned(c, cols)]
+            return whole.at[:, pl.ds(pl.multiple_of(c * stride + first, LANE), cols)]
 
         c = place.c
         self.own = pltpu.make_async_copy(half(c), to, local)
@@ -449,9 +417,10 @@
 
 
 class Line:
-    def __init__(self, place, nz, blk, land, left, move, got, total, out, sems, work):
+    def __init__(self, place, nz, blk, land, left, move, got, total, out, turned, sems, work):
         self.place, self.nz, self.blk = place, nz, blk
         self.land, self.left, self.move, self.got, self.total, self.out = land, left, move, got, total, out
+        self.turned = turned
         self.cols = land.shape[1]
         self.mv, self.lv, self.acc, self.stage, self.load_sem = work
         self.send, self.recv, self.end_s, self.end_r, self.end_l = sems
@@ -514,15 +483,28 @@
 
         lax.fori_loop(0, self.nz - 1, one, 0)
 
+    def sent(self):
+        def one(j, unused):
+            self.route(j)[4].wait_send()
+            return unused
+
+        lax.fori_loop(0, self.nz - 1, one, 0)
+
     def own_block(self):
         self.total[...] = self.product(self.place.z)
 
     def ends(self):
         half = self.blk // 2
         c, core = self.place.c, self.place.core
-        columns = self.out.at[:, aligned(c, self.cols)]
-        away = remote(self.total.at[aligned(1 - c, half), :], columns, self.end_s, self.end_r, core)
-        here = pltpu.make_async_copy(self.total.at[aligned(c, half), :], columns, self.end_l)
+        if self.turned is None:
+            to = self.out.at[:, aligned(c, self.cols)]
+            mine, theirs = self.total.at[aligned(c, half), :], self.total.at[aligned(1 - c, half), :]
+        else:
+            turned, stride, first = self.turned
+            to = self.out.at[pl.ds(pl.multiple_of(c * stride + first, LANE), self.cols), :]
+            mine, theirs = (turned.at[: self.cols, aligned(k, half)] for k in (c, 1 - c))
+        away = remote(theirs, to, self.end_s, self.end_r, core)
+        here = pltpu.make_async_copy(mine, to, self.end_l)
         return away, here
 
     def finish(self):
@@ -536,97 +518,242 @@
         def _():
             self.total[...] += self.take(nz)
 
+        if self.turned is not None:
+            self.turned[0][: self.cols, :] = jnp.transpose(self.total[...])
         for copy in self.ends():
             copy.start()
 
-    def drain(self):
-        def one(j, unused):
-            self.route(j)[4].wait_send()
+    def left_here(self):
+        away, here = self.ends()
+        away.wait_send()
+        here.wait()
+
+    def arrived(self):
+        self.ends()[0].wait_recv()
+
+
+class Weights:
+    def __init__(self, weights, buffers, sems, tail_sems, phase, cols, ff):
+        self.weights, self.buffers, self.sems, self.tail_sems, self.phase = weights, buffers, sems, tail_sems, phase
+        self.size = buffers.shape[1]
+        self.cols = cols
+        self.regular = 2 * (cols // self.size)
+        self.rest = cols % self.size
+        self.rest_two = ff - cols - cols // self.size * self.size
+
+    def slot(self, i, w):
+        return lax.rem(i + self.phase, 2) * 3 + w
+
+    def copies(self, i):
+        at = pl.ds(pl.multiple_of(lax.rem(i, 2) * self.cols + i // 2 * self.size, LANE), self.size)
+        return [
+            pltpu.make_async_copy(ref.at[at, :], self.buffers.at[self.slot(i, w)], self.sems.at[lax.rem(i, 2), w])
+            for w, ref in enumerate(self.weights)
+        ]
+
+    def tail(self):
+        first = self.cols // self.size * self.size
+        copies = []
+        for w, ref in enumerate(self.weights):
+            to = self.buffers.at[self.slot(self.regular, w)]
+            copies += [
+                pltpu.make_async_copy(ref.at[pl.ds(first, self.rest), :], to.at[pl.ds(0, self.rest), :], self.tail_sems.at[0, w]),
+                pltpu.make_async_copy(
+                    ref.at[pl.ds(self.cols + first, self.rest_two), :],
+                    to.at[pl.ds(self.rest, self.rest_two), :],
+                    self.tail_sems.at[1, w],
+                ),
+            ]
+        return copies
+
+    def begin(self):
+        for copy in self.copies(0):
+            copy.start()
+
+    def run(self, low, high, work):
+        def one(i, unused):
+            @pl.when(i + 1 < self.regular)
+            def _():
+                for copy in self.copies(i + 1):
+                    copy.start()
+
+            @pl.when(i + 1 == self.regular)
+            def _():
+                for copy in self.tail():
+                    copy.start()
+
+            for copy in self.copies(i):
+                copy.wait()
+            work([self.slot(i, w) for w in range(len(self.weights))], lax.rem(i, 2) * self.cols + i // 2 * self.size)
             return unused
 
-        lax.fori_loop(0, self.nz - 1, one, 0)
-        for copy in self.ends():
+        lax.fori_loop(low, high, one, 0)
+
+    def end(self, work):
+        for copy in self.tail():
             copy.wait()
+        slots = [(self.regular + self.phase) % 2 * 3 + w for w in range(len(self.weights))]
+        filled = self.rest + self.rest_two
+        for slot in slots:
+            self.buffers[slot, filled:, :] = jnp.zeros((self.size - filled, self.buffers.shape[2]), BF)
+        work(slots, None)
 
 
 def backward_kernel(
-    geo,
-    hidden, d_gate, d_up, d_two, mixed, left_cot, left_two, middle_in, x_in, cot_in, att_in,
+    geo, sizes,
+    wg_in, wu_in, wd_in, two_norm_in, left_cot, left_two, middle_in, x_in, cot_in, att_in,
     q_in, k_in, v_in, o_in, lse_in, seg_in, wo_in, wq_in, gain_one, gain_two,
-    ffn_in, input_grad, d_keys, d_values, gains,
+    ffn_own, ffn_in, input_grad, d_keys, d_values, gains,
     out_down, out_gate, out_up, out_out, out_query,
-    m_down, m_gate, m_up, m_out, m_query, l_two, l_err, l_one,
-    g_down, g_gate, g_up, g_out, g_query,
-    mid, x_all, cot_all, two_own, two_in, one_part, one_in, err, one, weight, d_att,
-    uq, uk, uv, uo, udo, lse, seg_all, seg_row, seg_col, k_t, delta, dk_acc, dv_acc, udq, udk, udv, dq,
+    m_down_a, m_down_b, m_gate, m_up, m_out, m_query, l_two, l_err, l_one,
+    g_down_a, g_down_b, g_gate, g_up, g_out, g_query,
+    mid, x_all, cot_all, two_norm, two_own, two_in, one_in, mixed, err, one, wbuf, d_att,
+    hidden, d_gate, d_up, sums,
+    uq, uk, uv, uo, udo, lse, seg_all, seg_row, seg_col, k_t, delta, udq, udk, udv, dq,
     gain_part, gain_in,
-    s_down, s_gate, s_up, s_out, s_query, t_down, t_gate, t_up, t_out, t_query,
+    s_first, s_second, s_out, s_query, t_first, t_second, t_out, t_query, turned,
     mv, lv, acc, stage,
-    tp_s, tp_r, a_s, a_r, me_s, me_r, le_s, le_r, c_s, c_r, e_s, e_r, e_l, loc, work_sem,
+    tp_s, tp_r, a_s, a_r, me_s, me_r, le_s, le_r, c_s, c_r, e_s, e_r, e_l, loc, work_sem, w_sem, tail_sem, o_sem,
 ):
     n, rows, tok, width, half, heads, length = geo
+    ff, cols, cols_a = sizes
     tokens = rows * tok
     blk = 2 * width // n
     nz = n // PLANE
     place = Place(n)
     s, t, z = place.s, place.t, place.z
     row_s, head_s = s // heads, lax.rem(s, heads)
-    place.enter()
     mine = aligned(t, half)
     chunk = tokens // 4
-
-    def two_copy(i):
-        at = aligned(i, chunk)
-        return remote(d_two.at[at, :], two_in.at[at, :], tp_s.at[i], tp_r.at[i], place.twin)
-
-    for i in range(4):
-        two_copy(i).start()
-    ffn_copy = remote(mixed.at[:, aligned(1 - t, half)], ffn_in, tp_s.at[4], tp_r.at[4], place.twin)
-    ffn_copy.start()
-
+    fine = 32
+    size = wbuf.shape[1]
+
+    first_pass = Weights((wg_in, wu_in, wd_in), wbuf, w_sem.at[0], tail_sem.at[0], 0, cols, ff)
+    second_pass = Weights((wg_in, wu_in), wbuf, w_sem.at[1], tail_sem.at[1], 1, cols, ff)
+    third_pass = Weights((wd_in,), wbuf, w_sem.at[2], tail_sem.at[2], 0, cols, ff)
+    first_pass.begin()
+    loads = [
+        pltpu.make_async_copy(a, b, loc.at[8 + i])
+        for i, (a, b) in enumerate((
+            (two_norm_in, two_norm), (cot_in, cot_all), (middle_in, mid), (x_in, x_all),
+            (q_in, uq), (k_in, uk), (v_in, uv), (o_in, uo), (lse_in, lse), (seg_in, seg_all),
+        ))
+    ]
+    for copy in loads[:2]:
+        copy.start()
+    place.enter()
+
+    rest_a = cols - cols_a
+    gather_of = (
+        (hidden, cols, 0, m_down_a), (hidden, cols, cols_a, m_down_b), (d_gate, cols, 0, m_gate), (d_up, cols, 0, m_up),
+        (att_in, half // 2, 0, m_out), (dq, half // 2, 0, m_query),
+    )
     gathers = [
-        Gather(place, whole, land, me_s.at[i], me_r.at[i], loc.at[i], tokens)
-        for i, (whole, land) in enumerate(
-            ((hidden, m_down), (d_gate, m_gate), (d_up, m_up), (att_in, m_out), (dq, m_query))
-        )
+        Gather(place, *refs, me_s.at[i], me_r.at[i], loc.at[i], tokens) for i, refs in enumerate(gather_of)
     ]
     lefts = [
-        Plane(place, split, land, le_s.at[i], le_r.at[i], loc.at[5 + i], tokens)
+        Plane(place, split, land, le_s.at[i], le_r.at[i], loc.at[25 + i], tokens)
         for i, (split, land) in enumerate(((left_two, l_two), (err, l_err), (one, l_one)))
     ]
     work = (mv, lv, acc, stage, work_sem)
+    first_a, first_b = pl.ds(0, cols_a), pl.ds(cols_a, rest_a)
     lines = [
         Line(place, nz, blk, *refs, (c_s.at[i], c_r.at[i], e_s.at[i], e_r.at[i], e_l.at[i]), work)
         for i, refs in enumerate((
-            (m_down, left_cot, s_down, g_down, t_down, out_down),
-            (m_gate, l_two, s_gate, g_gate, t_gate, out_gate),
-            (m_up, l_two, s_up, g_up, t_up, out_up),
-            (m_out, l_err, s_out, g_out, t_out, out_out),
-            (m_query, l_one, s_query, g_query, t_query, out_query),
+            (m_down_a, left_cot, s_first.at[:, :, first_a], g_down_a, t_first.at[:, first_a], out_down, (turned, cols, 0)),
+            (m_down_b, left_cot, s_first.at[:, :, first_b], g_down_b, t_first.at[:, first_b], out_down, (turned, cols, cols_a)),
+            (m_gate, l_two, s_second, g_gate, t_second, out_gate, (turned, cols, 0)),
+            (m_up, l_two, s_first, g_up, t_first, out_up, (turned, cols, 0)),
+            (m_out, l_err, s_out, g_out, t_out, out_out, None),
+            (m_query, l_one, s_query, g_query, t_query, out_query, None),
         ))
     ]
-    down, gate, up, out, query = lines
+    down_a, down_b, gate, up, out, query = lines
+
+    for copy in loads[:2]:
+        copy.wait()
+
+    def units(slots, at):
+        wg, wu, wd = (wbuf[slot] for slot in slots)
+        x, g = two_norm[...], cot_all[...]
+        gate_now, up_now = dot_nt(x, wg), dot_nt(x, wu)
+        d_hid = dot_nt(g, wd)
+        sigma = jax.nn.sigmoid(gate_now)
+        act = gate_now * sigma
+        for ref, now in (
+            (hidden, act * up_now),
+            (d_gate, d_hid * up_now * sigma * (1.0 + gate_now * (1.0 - sigma))),
+            (d_up, d_hid * act),
+        ):
+            now = now.astype(BF)
+            if at is None:
+                last, rest = cols // size * size, cols % size
+                ref[:, last:cols] = now[:, :rest]
+                ref[:, cols + last :] = now[:, rest : 2 * rest]
+            else:
+                ref[:, pl.ds(pl.multiple_of(at, LANE), size)] = now
+
+    first_pass.run(0, 2 * (cols_a // size), units)
     gathers[0].start()
-
-    loads = [
-        pltpu.make_async_copy(a, b, loc.at[8 + i])
-        for i, (a, b) in enumerate((
-            (middle_in, mid), (d_two, two_own), (cot_in, cot_all), (wo_in, weight), (x_in, x_all),
-            (q_in, uq), (k_in, uk), (v_in, uv), (o_in, uo), (lse_in, lse), (seg_in, seg_all),
-        ))
-    ]
-    for copy in loads:
+    first_pass.run(2 * (cols_a // size), first_pass.regular, units)
+    second_pass.begin()
+    first_pass.end(units)
+    gathers[1].start()
+    lefts[0].start()
+    for copy in loads[2:]:
         copy.start()
-    for copy in loads[:4]:
-        copy.wait()
+
+    def block_of(ref, at):
+        if at is None:
+            last, rest = cols // size * size, cols % size
+            return jnp.concatenate([ref[:, last:cols], ref[:, cols + last :]], axis=1)
+        return ref[:, pl.ds(pl.multiple_of(at, LANE), size)]
+
+    def add_up(pairs):
+        for db in range(width // size):
+            at = slice(db * size, (db + 1) * size)
+            sums[db * tokens : (db + 1) * tokens, :] += sum(dot_nn(a, wbuf[slot, :, at]) for a, slot in pairs)
+
+    def back_units(slots, at):
+        add_up([(block_of(d_gate, at), slots[0]), (block_of(d_up, at), slots[1])])
+
+    sums[...] = jnp.zeros_like(sums)
+    second_pass.run(0, second_pass.regular, back_units)
+    second_pass.end(back_units)
+    for db in range(width // size):
+        two_own[:, db * size : (db + 1) * size] = sums[db * tokens : (db + 1) * tokens, :].astype(BF)
+
+    def two_copy(i):
+        at = aligned(i, chunk)
+        return remote(two_own.at[at, :], two_in.at[at, :], tp_s.at[i], tp_r.at[i], place.twin)
+
+    for i in range(4):
+        two_copy(i).start()
+    load_square = []
+    for k, ref in enumerate((wo_in, wq_in)):
+        for zy in range(n // 2):
+            to = wbuf.at[4 * k + zy // 2, :, (zy % 2) * half : (zy % 2 + 1) * half]
+            load_square.append(pltpu.make_async_copy(ref.at[zy * blk : (zy + 1) * blk, :], to, o_sem.at[k, zy]))
+    for copy in load_square:
+        copy.start()
+
+    def square_block(k, zy):
+        return wbuf[4 * k + zy // 2, :, (zy % 2) * half : (zy % 2 + 1) * half]
+
+    gathers[0].wait()
+    down_a.load(True)
+    down_a.steps()
+    down_a.own_block()
 
     spread_att = Spread(
         place,
         lambda d: d_att.at[aligned(d // heads, tok), aligned(lax.rem(d, heads), HEAD_DIM)],
         lambda: udo.at[aligned(s, tok), :],
-        a_s.at[0], a_r.at[0], loc.at[19],
-    )
-    fine = 32
+        a_s.at[0], a_r.at[0], loc.at[18],
+    )
+    loads[2].wait()
+    for copy in load_square[: n // 2]:
+        copy.wait()
 
     def second_norm(i, gain_sum):
         two_copy(i).wait()
@@ -653,7 +780,7 @@
         total = jnp.zeros((chunk, half), F32)
         for zy in range(n // 2):
             zz, yy = divmod(zy, 2)
-            total += dot_nn(err[yy, at, zz * blk : (zz + 1) * blk], weight[zy * blk : (zy + 1) * blk, :])
+            total += dot_nn(err[yy, at, zz * blk : (zz + 1) * blk], square_block(0, zy))
         d_att[at, :] = total.astype(BF)
         return gain_sum
 
@@ -665,20 +792,43 @@
     for i in range(n):
         gain_part[0, i] = gain_sum[:, i * (width // n) : (i + 1) * (width // n)]
     spread_gain = [
-        Spread(place, lambda d, g=g: gain_part.at[g, d], lambda g=g: gain_in.at[g, s], a_s.at[4 + g], a_r.at[4 + g], loc.at[23 + g])
+        Spread(place, lambda d, g=g: gain_part.at[g, d], lambda g=g: gain_in.at[g, s], a_s.at[4 + g], a_r.at[4 + g], loc.at[22 + g])
         for g in range(2)
     ]
     spread_gain[0].start()
-    load_q = pltpu.make_async_copy(wq_in, weight, loc.at[25])
-    load_q.start()
-
-    lefts[0].start()
-    gathers[1].start()
+    lefts[0].forward()
     gathers[2].start()
+    gathers[3].start()
     lefts[1].start()
-    gathers[3].start()
-
-    loads[4].wait()
+    gathers[4].start()
+
+    gathers[1].wait()
+    down_b.load(False)
+    at_end = (z == 0) | (z == nz - 1)
+
+    @pl.when(at_end)
+    def _():
+        down_b.steps()
+
+    down_b.own_block()
+
+    third_pass.begin()
+    sums[...] = jnp.zeros_like(sums)
+
+    def out_units(slots, at):
+        add_up([(block_of(hidden, at), slots[0])])
+
+    third_pass.run(0, third_pass.regular, out_units)
+    third_pass.end(out_units)
+    for db in range(width // size):
+        mixed[:, db * size : (db + 1) * size] = sums[db * tokens : (db + 1) * tokens, :].astype(BF)
+    ffn_copy = remote(mixed.at[:, aligned(1 - t, half)], ffn_in, tp_s.at[4], tp_r.at[4], place.twin)
+    ffn_copy.start()
+    ffn_keep = pltpu.make_async_copy(mixed.at[:, mine], ffn_own, loc.at[6])
+    ffn_keep.start()
+
+    for copy in loads[3:]:
+        copy.wait()
 
     def first_norm(j, unused):
         at = aligned(j, fine)
@@ -691,9 +841,6 @@
         return unused
 
     lax.fori_loop(0, tokens // fine, first_norm, 0)
-
-    for copy in loads[5:]:
-        copy.wait()
     attention_masks(seg_all, seg_row, seg_col, n, tok)
 
     def turn(i, unused):
@@ -702,16 +849,7 @@
         return unused
 
     lax.fori_loop(0, n, turn, 0)
-    dk_acc[...] = jnp.zeros_like(dk_acc)
-    dv_acc[...] = jnp.zeros_like(dv_acc)
-
-    gathers[0].wait()
-    down.load(True)
-    at_end = (z == 0) | (z == nz - 1)
-
-    @pl.when(at_end)
-    def _():
-        down.steps()
+    sums[...] = jnp.zeros_like(sums)
 
     spread_att.wait()
 
@@ -730,7 +868,7 @@
         return lambda: ref.at[aligned(row_s, tok), aligned(head_s, HEAD_DIM)]
 
     spread_dq, spread_dk, spread_dv = (
-        Spread(place, lambda d, unit=unit: unit.at[aligned(d, tok), :], home(whole), a_s.at[i], a_r.at[i], loc.at[19 + i])
+        Spread(place, lambda d, unit=unit: unit.at[aligned(d, tok), :], home(whole), a_s.at[i], a_r.at[i], loc.at[18 + i])
         for i, unit, whole in ((1, udq, dq), (2, udk, d_keys), (3, udv, d_values))
     )
 
@@ -745,15 +883,15 @@
             probs = jnp.exp(jnp.where(readable(seg_col, seg_row, kj, qi, block), scores, NEGATIVE_FILL))
             d_probs = dot_nt(uv[kat, :], dob)
             d_scores = (probs * (d_probs - delta[:, qat])).astype(BF)
-            dv_acc[kat, :] += dot_nn(probs.astype(BF), dob)
-            dk_acc[kat, :] += dot_nn(d_scores, qb)
+            sums[kat, :HEAD_DIM] += dot_nn(d_scores, qb)
+            sums[kat, HEAD_DIM:] += dot_nn(probs.astype(BF), dob)
             return dq_t + dot_nn(k_t[:, kat], d_scores)
 
         dq_t = lax.fori_loop(0, qi + 1, key_step, jnp.zeros((HEAD_DIM, block), F32))
         udq[qat, :] = jnp.transpose(dq_t).astype(BF)
         lax.fori_loop(qi * owners, (qi + 1) * owners, spread_dq.start_to, 0)
-        udk[qat, :] = dk_acc[qat, :].astype(BF)
-        udv[qat, :] = dv_acc[qat, :].astype(BF)
+        udk[qat, :] = sums[qat, :HEAD_DIM].astype(BF)
+        udv[qat, :] = sums[qat, HEAD_DIM:].astype(BF)
         lax.fori_loop(qi * owners, (qi + 1) * owners, spread_dk.start_to, 0)
         lax.fori_loop(qi * owners, (qi + 1) * owners, spread_dv.start_to, 0)
         return unused
@@ -762,40 +900,44 @@
 
     @pl.when(jnp.logical_not(at_end))
     def _():
-        down.steps()
-
-    down.own_block()
-    lefts[0].forward()
-    gathers[1].wait()
+        down_b.steps()
+
+    down_a.finish()
+    gathers[2].wait()
     lefts[0].finish()
     gate.load(True)
     gate.steps()
     gate.own_block()
-
-    load_q.wait()
+    down_a.left_here()
+    down_b.finish()
+
+    for copy in load_square[n // 2 :]:
+        copy.wait()
     spread_dq.wait()
-    gathers[4].start()
+    gathers[5].start()
     lefts[2].start()
+    lefts[1].forward()
 
     def one_copy(i):
         at = aligned(i, chunk)
-        return remote(one_part.at[at, :], one_in.at[at, :], tp_s.at[5 + i], tp_r.at[5 + i], place.twin)
+        return remote(two_own.at[at, :], one_in.at[at, :], tp_s.at[5 + i], tp_r.at[5 + i], place.twin)
 
     def back_query(i, unused):
         at = aligned(i, chunk)
-        one_part[at, :] = (dot_nt(dq[at, :], weight[...]) * HEAD_DIM ** (-0.5)).astype(BF)
+        for zy in range(n // 2):
+            now = dot_nt(dq[at, :], square_block(1, zy)) * HEAD_DIM ** (-0.5)
+            two_own[at, zy * blk : (zy + 1) * blk] = now.astype(BF)
         one_copy(i).start()
         return unused
 
     lax.fori_loop(0, 4, back_query, 0)
 
-    gathers[2].wait()
+    gathers[3].wait()
+    down_a.sent()
+    down_b.sent()
     up.load(False)
     up.steps()
     up.own_block()
-    down.finish()
-
-    lefts[1].forward()
 
     def last_norm(i, gain_sum):
         one_copy(i).wait()
@@ -803,7 +945,7 @@
         def some(j, gain_sum):
             at = aligned(i * (chunk // fine) + j, fine)
             x = x_all[at, :].astype(F32)
-            d1 = one_part[at, :].astype(F32) + one_in[at, :].astype(F32)
+            d1 = two_own[at, :].astype(F32) + one_in[at, :].astype(F32)
             root = lax.rsqrt(jnp.mean(x * x, axis=-1, keepdims=True) + EPSILON)
             gained = d1 * gain_one[...]
             scaled = x * root
@@ -818,22 +960,24 @@
     for i in range(n):
         gain_part[1, i] = gain_sum[:, i * (width // n) : (i + 1) * (width // n)]
     spread_gain[1].start()
-    give = pltpu.make_async_copy(mid.at[:, mine], input_grad, loc.at[26])
+    give = pltpu.make_async_copy(mid.at[:, mine], input_grad, loc.at[24])
     give.start()
 
-    gathers[3].wait()
+    gathers[4].wait()
     lefts[1].finish()
+    lefts[2].forward()
     out.load(True)
     out.steps()
     out.own_block()
-    gate.finish()
-
-    lefts[2].forward()
-    gathers[4].wait()
+
+    gathers[5].wait()
     lefts[2].finish()
     query.load(True)
     query.steps()
     query.own_block()
+    down_b.left_here()
+    gate.finish()
+    gate.left_here()
     up.finish()
     out.finish()
     query.finish()
@@ -844,66 +988,79 @@
         spread_gain[g].wait()
         gains[g] = jnp.sum(gain_in[g], axis=0)
     ffn_copy.wait()
+    ffn_keep.wait()
     give.wait()
+    for line in lines[2:]:
+        line.sent()
+    for line in lines[3:]:
+        line.left_here()
     for line in lines:
-        line.drain()
-
-
-def backward_part(geo, ffn, forward, wo, wq, gain_one, gain_two):
+        line.arrived()
+
+
+def backward_part(geo, forward, wg, wu, wd, wo, wq, gain_one, gain_two):
     n, rows, tok, width, half, heads, length = geo
     tokens = rows * tok
     blk = 2 * width // n
     nz = n // PLANE
-    hidden, d_gate, d_up, d_two, mixed = ffn
-    x_all, cot_all, left_cot, middle, _, left_two, attended, uq, uk, uv, uo, lse, seg_all = forward
+    ff = wg.shape[0]
+    size = 2 * LANE
+    cols = -(-ff // size) * LANE
+    cols_a = cols // size * size // 2 // size * size + (size if cols // size % 2 else 0)
+    sizes = (ff, cols, cols_a)
+    x_all, cot_all, left_cot, middle, normed_two, left_two, attended, uq, uk, uv, uo, lse, seg_all = forward
     dma = pltpu.SemaphoreType.DMA
     anywhere, here = pl.BlockSpec(memory_space=pl.ANY), pl.BlockSpec(memory_space=pltpu.VMEM)
-    wide = (hidden.shape[1] // 2,) * 3 + (half // 2,) * 2
+    wide = (cols_a, cols - cols_a, cols, cols, half // 2, half // 2)
     outs = [
+        (vm((tokens, half), BF), anywhere),
         (vm((tokens, half), BF), anywhere),
         (vm((tokens, half), F32), anywhere),
         (vm((tokens, half), BF), anywhere),
         (vm((tokens, half), BF), anywhere),
         (vm((2, 1, width // n), F32), here),
-        *((vm((blk // 2, 2 * cols), F32), anywhere) for cols in wide),
-        *((vm((PLANE * tokens, cols), BF), anywhere) for cols in wide),
+        *((vm((2 * cols, blk // 2), F32), anywhere) for _ in range(3)),
+        *((vm((blk // 2, half), F32), anywhere) for _ in range(2)),
+        *((vm((PLANE * tokens, c), BF), anywhere) for c in wide),
         *((vm((PLANE * tokens, width // 2), BF), anywhere) for _ in range(3)),
-        *((vm((nz + 1, blk, cols), BF), anywhere) for cols in wide),
+        *((vm((nz + 1, blk, c), BF), anywhere) for c in wide),
     ]
     inputs = [
-        hidden, d_gate, d_up, d_two, mixed, left_cot, left_two, middle, x_all, cot_all, attended,
+        wg, wu, wd, normed_two, left_cot, left_two, middle, x_all, cot_all, attended,
         uq, uk, uv, uo, lse, seg_all, wo, wq, gain_one, gain_two,
     ]
-    big = max(wide)
     unit = pltpu.VMEM((length, HEAD_DIM), BF)
-    unit_sum = pltpu.VMEM((length, HEAD_DIM), F32)
     line = pltpu.VMEM((1, length), F32)
     act = pltpu.VMEM((tokens, width), BF)
     split = pltpu.VMEM((2, tokens, width // 2), BF)
+    hid = pltpu.VMEM((tokens, 2 * cols), BF)
     scratch = [
-        pltpu.VMEM((tokens, width), F32), act, act, act, act, act, act, split, split,
-        pltpu.VMEM(wo.shape, BF), pltpu.VMEM((tokens, half), BF),
+        pltpu.VMEM((tokens, width), F32), act, act, act, act, act, act, act, split, split,
+        pltpu.VMEM((8, size, width), BF), pltpu.VMEM((tokens, half), BF),
+        hid, hid, hid, pltpu.VMEM((length, size), F32),
         unit, unit, unit, unit, unit, line, pltpu.VMEM((n, 1, tok), F32), line,
         pltpu.VMEM((length, LANE), F32), pltpu.VMEM((HEAD_DIM, length), BF), line,
-        unit_sum, unit_sum, unit, unit, unit, pltpu.VMEM((tokens, half), BF),
+        unit, unit, unit, pltpu.VMEM((tokens, half), BF),
         pltpu.VMEM((2, n, 1, width // n), F32), pltpu.VMEM((2, n, 1, width // n), F32),
-        *(pltpu.VMEM((nz - 1, blk, cols), BF) for cols in wide),
-        *(pltpu.VMEM((blk, cols), F32) for cols in wide),
-        pltpu.VMEM((PLANE * tokens, big), BF), pltpu.VMEM((PLANE * tokens, width // 2), BF),
-        pltpu.VMEM((blk, big), F32), pltpu.VMEM((blk, big), BF),
-        dma((9,)), dma((9,)), dma((6, n)), dma((6, n)), dma((5, 3)), dma((5, 3)), dma((3, 3)), dma((3, 3)),
-        dma((5, nz - 1)), dma((5, nz + 1)), dma((5,)), dma((5,)), dma((5,)), dma((27,)), dma((3,)),
+        *(pltpu.VMEM((nz - 1, blk, c), BF) for c in wide[2:]),
+        *(pltpu.VMEM((blk, c), F32) for c in wide[2:]),
+        pltpu.VMEM((cols, blk), F32),
+        pltpu.VMEM((PLANE * tokens, cols), BF), pltpu.VMEM((PLANE * tokens, width // 2), BF),
+        pltpu.VMEM((blk, cols), F32), pltpu.VMEM((blk, cols), BF),
+        dma((9,)), dma((9,)), dma((6, n)), dma((6, n)), dma((6, 3)), dma((6, 3)), dma((3, 3)), dma((3, 3)),
+        dma((6, nz - 1)), dma((6, nz + 1)), dma((6,)), dma((6,)), dma((6,)), dma((28,)), dma((3,)),
+        dma((3, 2, 3)), dma((3, 2, 3)), dma((2, n // 2)),
     ]
     return pl.pallas_call(
-        functools.partial(backward_kernel, geo),
+        functools.partial(backward_kernel, geo, sizes),
         out_shape=[o for o, _ in outs],
         in_specs=[anywhere] * (len(inputs) - 2) + [here] * 2,
         out_specs=[spec for _, spec in outs],
         scratch_shapes=scratch,
         compiler_params=pltpu.CompilerParams(
-            collective_id=1, has_side_effects=True, vmem_limit_bytes=62 * MIB
+            collective_id=1, has_side_effects=True, vmem_limit_bytes=VMEM_GRANT
         ),
-        name="backward",
+        name="feed_forward_and_backward",
     )(*inputs)
 
 
@@ -915,7 +1072,6 @@
     tokens, width, ff = rows * tok, query_weight.shape[0], gate_weight.shape[1]
     heads = half // HEAD_DIM
     geo = (n, rows, tok, width, half, heads, n * tok)
-    padded = -(-ff // (2 * LANE)) * 2 * LANE
 
     def flat(a):
         return a.reshape(tokens, half)
@@ -925,16 +1081,12 @@
     forward = forward_part(
         geo, flat(inputs), flat(cotangent), flat(keys), flat(values), segf, gain_one, gain_two, query_weight, out_weight
     )
-    x_all, cot_all, _, middle, normed_two = forward[:5]
-    ffn = ffn_part(padded, normed_two, cot_all, gate_weight, up_weight, down_weight)
-    back = backward_part(geo, ffn, forward, out_weight, query_weight, gain_one, gain_two)
-    ffn_in, input_grad, d_keys, d_values, gains, g_down, g_gate, g_up, g_out, g_query = back[:10]
-    at = lax.axis_index("tp") * half
-    mixed = (
-        lax.dynamic_slice_in_dim(middle, at, half, 1)
-        + lax.dynamic_slice_in_dim(ffn[4], at, half, 1).astype(F32)
-        + ffn_in.astype(F32)
-    ).astype(BF)
+    back = backward_part(
+        geo, forward, gate_weight.T, up_weight.T, down_weight.T, out_weight, query_weight, gain_one, gain_two
+    )
+    ffn_own, ffn_in, input_grad, d_keys, d_values, gains, g_down, g_gate, g_up, g_out, g_query = back[:11]
+    middle = lax.dynamic_slice_in_dim(forward[3], lax.axis_index("tp") * half, half, 1)
+    mixed = (middle + ffn_own.astype(F32) + ffn_in.astype(F32)).astype(BF)
 
     def shaped(a):
         return a.reshape(rows, tok, half)
@@ -948,9 +1100,9 @@
         g_query * HEAD_DIM ** (-0.5),
         g_out,
         gains[0, 0],
-        g_gate[:, :ff],
-        g_up[:, :ff],
-        g_down[:, :ff],
+        g_gate[:ff].T,
+        g_up[:ff].T,
+        g_down[:ff].T,
     )
 
 

time: 457 us -> 377 us (0.82)
  local copies, waits for them, and re-layouts: 68.9 us -> 7.11 us
  Pallas kernels: 377 us -> 357 us
    unnamed x62 -> x20, local copies, waits for them, and re-layouts: 68.4 us -> 1.8 us
    pallas_call x2 -> x1, Pallas kernels: 297 us -> 277 us  [backward_part(): pl.pallas_call(functools.partial(backward_kernel, geo, sizes), out_shape=...]
    transpose x0 -> x2, local copies, waits for them, and re-layouts: none -> 4.8 us  [the longest x1 3.62 us: fast_device(): g_down[:ff]]
where the time goes in v2:
time: 377 us; the launch traced here: 371 us
  Pallas kernels  357 us (95%)
  local copies, waits for them, and re-layouts  7.11 us (2%)
  other arithmetic  6.45 us (2%)
    pallas_call x1, Pallas kernels, backward_part(): pl.pallas_call(functools.partial(backward_kernel, geo, sizes), out_shape=...  277 us
    pallas_call x1, Pallas kernels, forward_part(): pl.pallas_call(functools.partial(forward_kernel, geo), out_shape=outs, in...  80.4 us

profile of v2, /device:TPU:0, one launch (start us, length us, event | category | flops | bytes accessed | tf_op | source)
XLA Modules:
  0.0 371.3 jit_solution(16525111077329914325)
XLA Ops:
  0.6 1.2 convert_element_type.14
  1.9 80.4 %attention_forward.1 = (bf16[256,2048]{1,0:T(8,128)(2,1)}, bf16[256,2048]{1,0:T(8,128)(2,1)}, bf16[1024,1024]{1,0:T(8,128)(2,1)}, f32[256,2048]{1,0:T(8,128)}, b...) custom-call(bf16[256,1024]{1,0:T(8,128)(2,1)} %bitcast.33, ...), custom_call_target="tpu_custom_call" | custom-call | tf_op jit(solution)/shard_map/attention_forward/pallas_call | solution.py:366
  82.3 276.6 %feed_forward_and_backward.1 = (bf16[256,1024]{1,0:T(8,128)(2,1)}, bf16[256,1024]{1,0:T(8,128)(2,1)}, f32[256,1024]{1,0:T(8,128)}, bf16[256,1024]{1,0:T(8,128)(2...) custom-call(bf16[2752,2048]{1,0:T(8,128)(2,1)} %bitcast.26, ...), custom_call_target="tpu_custom_call" | custom-call | tf_op jit(solution)/shard_map/feed_forward_and_backward/pallas_call | solution.py:1054
  358.9 0.0 copy-start.1
  358.9 3.6 slice_bitcast_fusion
  362.6 0.0 copy-start.4
  362.6 0.0 copy-done.1
  362.6 0.0 copy-start.3
  362.6 1.2 slice_bitcast_fusion.2
  363.8 0.0 copy-start
  363.8 0.0 copy-start.7
  363.8 0.0 copy-done.4
  363.8 1.1 convert.2
  364.9 0.0 copy-done.3
  364.9 1.1 convert.3
  365.9 0.0 copy-start.6
  365.9 0.0 copy-done
  365.9 0.0 copy-done.7
  365.9 0.0 copy-start.8
  366.0 0.0 copy-start.2
  366.0 2.2 add_convert_fusion
  368.2 0.0 copy-start.5
  368.2 0.0 copy-done.6
  368.2 0.8 broadcast_multiply_fusion
  369.0 0.0 copy-done.8
  369.0 0.5 slice_bitcast_fusion.3
  369.5 0.0 copy-done.2
  369.5 1.0 copy.25
  370.5 0.0 copy-done.5
  370.5 0.8 copy.26
Async XLA Ops:
  358.9 3.6 copy-start.1
  362.6 1.2 copy-start.4
  362.6 2.3 copy-start.3
  363.8 2.2 copy-start
  363.8 2.2 copy-start.7
  365.9 2.2 copy-start.6
  365.9 3.1 copy-start.8
  366.0 3.6 copy-start.2
  368.2 2.3 copy-start.5

commit v3 on v2

--- a/solution.py
+++ b/solution.py
@@ -417,16 +417,19 @@
 
 
 class Line:
-    def __init__(self, place, nz, blk, land, left, move, got, total, out, turned, sems, work):
-        self.place, self.nz, self.blk = place, nz, blk
+    def __init__(self, place, nz, blk, gather, land, left, lv, mv, move, got, total, out, turned, sems, work):
+        self.place, self.nz, self.blk, self.gather = place, nz, blk, gather
         self.land, self.left, self.move, self.got, self.total, self.out = land, left, move, got, total, out
         self.turned = turned
         self.cols = land.shape[1]
-        self.mv, self.lv, self.acc, self.stage, self.load_sem = work
+        self.lv, self.mv = lv, mv
+        self.acc, self.stage, self.load_sem = work
         self.send, self.recv, self.end_s, self.end_r, self.end_l = sems
-
-    def load(self, left_too):
-        a = pltpu.make_async_copy(self.land, self.mv.at[:, : self.cols], self.load_sem.at[0])
+        self.at_end = (place.z == 0) | (place.z == nz - 1)
+
+    def load(self, left_too=False):
+        self.gather.wait()
+        a = pltpu.make_async_copy(self.land, self.mv, self.load_sem.at[0])
         a.start()
         if left_too:
             b = pltpu.make_async_copy(self.left, self.lv, self.load_sem.at[1])
@@ -435,7 +438,7 @@
         a.wait()
 
     def product(self, b):
-        return dot_tn(self.lv[:, aligned(b, self.blk)], self.mv[:, : self.cols])
+        return dot_tn(self.lv[:, aligned(b, self.blk)], self.mv[...])
 
     def take(self, slot):
         self.arrival(slot).wait_recv()
@@ -459,7 +462,10 @@
         keep = jnp.where(up, b - 1, b)
         last = jnp.where(up, z == 0, z == nz - 1)
         device = (to * PLANE + self.place.p, self.place.t)
-        out = remote(self.move.at[keep], self.got.at[slot_out], self.send.at[keep], self.recv.at[slot_out], device)
+
+        def out():
+            return remote(self.move.at[keep], self.got.at[slot_out], self.send.at[keep], self.recv.at[slot_out], device)
+
         return b, slot_in, keep, last, out
 
     def step(self, j):
@@ -474,38 +480,45 @@
         def _():
             self.move[keep] = (self.acc[:, : self.cols] + self.take(slot_in)).astype(BF)
 
-        out.start()
-
-    def steps(self):
+        out().start()
+
+    def steps(self, low, high):
         def one(j, unused):
             self.step(j)
             return unused
 
-        lax.fori_loop(0, self.nz - 1, one, 0)
+        lax.fori_loop(low, high, one, 0)
+
+    def from_end(self):
+        pl.when(self.at_end)(lambda: self.steps(0, self.nz - 1))
+        self.total[...] = self.product(self.place.z)
+
+    def between(self, low, high):
+        pl.when(jnp.logical_not(self.at_end))(lambda: self.steps(low, high))
 
     def sent(self):
         def one(j, unused):
-            self.route(j)[4].wait_send()
+            self.route(j)[4]().wait_send()
             return unused
 
         lax.fori_loop(0, self.nz - 1, one, 0)
 
-    def own_block(self):
-        self.total[...] = self.product(self.place.z)
-
-    def ends(self):
+    def end(self, c):
         half = self.blk // 2
-        c, core = self.place.c, self.place.core
+        mine = self.place.c
         if self.turned is None:
-            to = self.out.at[:, aligned(c, self.cols)]
-            mine, theirs = self.total.at[aligned(c, half), :], self.total.at[aligned(1 - c, half), :]
-        else:
-            turned, stride, first = self.turned
-            to = self.out.at[pl.ds(pl.multiple_of(c * stride + first, LANE), self.cols), :]
-            mine, theirs = (turned.at[: self.cols, aligned(k, half)] for k in (c, 1 - c))
-        away = remote(theirs, to, self.end_s, self.end_r, core)
-        here = pltpu.make_async_copy(mine, to, self.end_l)
-        return away, here
+            return self.out.at[:, aligned(mine, self.cols)], self.total.at[aligned(c, half), :]
+        turned, stride, first = self.turned
+        to = self.out.at[pl.ds(pl.multiple_of(mine * stride + first, LANE), self.cols), :]
+        return to, turned.at[first : first + self.cols, aligned(c, half)]
+
+    def away(self):
+        to, theirs = self.end(1 - self.place.c)
+        return remote(theirs, to, self.end_s, self.end_r, self.place.core)
+
+    def here(self):
+        to, mine = self.end(self.place.c)
+        return pltpu.make_async_copy(mine, to, self.end_l)
 
     def finish(self):
         z, nz = self.place.z, self.nz
@@ -519,22 +532,23 @@
             self.total[...] += self.take(nz)
 
         if self.turned is not None:
-            self.turned[0][: self.cols, :] = jnp.transpose(self.total[...])
-        for copy in self.ends():
-            copy.start()
+            turned, _, first = self.turned
+            turned[first : first + self.cols, :] = jnp.transpose(self.total[...])
+        self.away().start()
+        self.here().start()
 
     def left_here(self):
-        away, here = self.ends()
-        away.wait_send()
-        here.wait()
+        self.away().wait_send()
+        self.here().wait()
 
     def arrived(self):
-        self.ends()[0].wait_recv()
+        self.away().wait_recv()
 
 
 class Weights:
-    def __init__(self, weights, buffers, sems, tail_sems, phase, cols, ff):
+    def __init__(self, weights, buffers, sems, tail_sems, phase, first, cols, ff):
         self.weights, self.buffers, self.sems, self.tail_sems, self.phase = weights, buffers, sems, tail_sems, phase
+        self.first, self.each = first, len(weights)
         self.size = buffers.shape[1]
         self.cols = cols
         self.regular = 2 * (cols // self.size)
@@ -542,7 +556,7 @@
         self.rest_two = ff - cols - cols // self.size * self.size
 
     def slot(self, i, w):
-        return lax.rem(i + self.phase, 2) * 3 + w
+        return self.first + lax.rem(i + self.phase, 2) * self.each + w
 
     def copies(self, i):
         at = pl.ds(pl.multiple_of(lax.rem(i, 2) * self.cols + i // 2 * self.size, LANE), self.size)
@@ -592,7 +606,7 @@
     def end(self, work):
         for copy in self.tail():
             copy.wait()
-        slots = [(self.regular + self.phase) % 2 * 3 + w for w in range(len(self.weights))]
+        slots = [self.first + (self.regular + self.phase) % 2 * self.each + w for w in range(self.each)]
         filled = self.rest + self.rest_two
         for slot in slots:
             self.buffers[slot, filled:, :] = jnp.zeros((self.size - filled, self.buffers.shape[2]), BF)
@@ -605,18 +619,21 @@
     q_in, k_in, v_in, o_in, lse_in, seg_in, wo_in, wq_in, gain_one, gain_two,
     ffn_own, ffn_in, input_grad, d_keys, d_values, gains,
     out_down, out_gate, out_up, out_out, out_query,
-    m_down_a, m_down_b, m_gate, m_up, m_out, m_query, l_two, l_err, l_one,
-    g_down_a, g_down_b, g_gate, g_up, g_out, g_query,
-    mid, x_all, cot_all, two_norm, two_own, two_in, one_in, mixed, err, one, wbuf, d_att,
-    hidden, d_gate, d_up, sums,
-    uq, uk, uv, uo, udo, lse, seg_all, seg_row, seg_col, k_t, delta, udq, udk, udv, dq,
-    gain_part, gain_in,
-    s_first, s_second, s_out, s_query, t_first, t_second, t_out, t_query, turned,
-    mv, lv, acc, stage,
-    tp_s, tp_r, a_s, a_r, me_s, me_r, le_s, le_r, c_s, c_r, e_s, e_r, e_l, loc, work_sem, w_sem, tail_sem, o_sem,
+    *rest,
 ):
     n, rows, tok, width, half, heads, length = geo
-    ff, cols, cols_a = sizes
+    ff, cols, cuts = sizes
+    n_lines = len(cuts) + 2
+    lands, (l_two, l_err, l_one), gots = rest[:n_lines], rest[n_lines : n_lines + 3], rest[n_lines + 3 : 2 * n_lines + 3]
+    (
+        mid, x_all, cot_all, two_norm, two_own, two_in, one_in, mixed, err, one, wbuf, d_att,
+        hidden, d_gate, d_up, sums,
+        uq, uk, uv, uo, udo, lse, seg_all, seg_row, seg_col, k_t, delta, udq, udk, udv, dq,
+        gain_part, gain_in,
+        s_first, s_second, s_out, s_query, t_first, t_second, t_out, t_query, turned,
+        mv, mv_out, mv_query, lv_one, lv_two, acc, stage,
+        tp_s, tp_r, a_s, a_r, me_s, me_r, le_s, le_r, c_s, c_r, e_s, e_r, e_l, loc, g_loc, work_sem, w_sem, tail_sem, o_sem,
+    ) = rest[2 * n_lines + 3 :]
     tokens = rows * tok
     blk = 2 * width // n
     nz = n // PLANE
@@ -628,9 +645,9 @@
     fine = 32
     size = wbuf.shape[1]
 
-    first_pass = Weights((wg_in, wu_in, wd_in), wbuf, w_sem.at[0], tail_sem.at[0], 0, cols, ff)
-    second_pass = Weights((wg_in, wu_in), wbuf, w_sem.at[1], tail_sem.at[1], 1, cols, ff)
-    third_pass = Weights((wd_in,), wbuf, w_sem.at[2], tail_sem.at[2], 0, cols, ff)
+    first_pass = Weights((wg_in, wu_in, wd_in), wbuf, w_sem.at[0], tail_sem.at[0], 0, 0, cols, ff)
+    second_pass = Weights((wg_in, wu_in), wbuf, w_sem.at[1], tail_sem.at[1], 0, 3, cols, ff)
+    third_pass = Weights((wd_in,), wbuf, w_sem.at[2], tail_sem.at[2], 0, 4, cols, ff)
     first_pass.begin()
     loads = [
         pltpu.make_async_copy(a, b, loc.at[8 + i])
@@ -643,32 +660,33 @@
         copy.start()
     place.enter()
 
-    rest_a = cols - cols_a
-    gather_of = (
-        (hidden, cols, 0, m_down_a), (hidden, cols, cols_a, m_down_b), (d_gate, cols, 0, m_gate), (d_up, cols, 0, m_up),
-        (att_in, half // 2, 0, m_out), (dq, half // 2, 0, m_query),
-    )
-    gathers = [
-        Gather(place, *refs, me_s.at[i], me_r.at[i], loc.at[i], tokens) for i, refs in enumerate(gather_of)
-    ]
+    work = (acc, stage, work_sem)
+    sources = {"down": hidden, "gate": d_gate, "up": d_up}
+    lefts_of = {"down": (left_cot, lv_one), "gate": (l_two, lv_two), "up": (l_two, lv_two)}
+    kept = {"down": (s_first, t_first, out_down), "gate": (s_second, t_second, out_gate), "up": (s_first, t_first, out_up)}
+    plans = []
+    for kind, first, wide in cuts:
+        at = pl.ds(first, wide)
+        left, lv = lefts_of[kind]
+        move, total, out_ref = kept[kind]
+        plans.append((
+            (sources[kind], cols, first), left, lv, mv.at[:, at], move.at[:, :, at], total.at[:, at], out_ref,
+            (turned, cols, first),
+        ))
+    plans.append(((att_in, half // 2, 0), l_err, lv_one, mv_out, s_out, t_out, out_out, None))
+    plans.append(((dq, half // 2, 0), l_one, lv_two, mv_query, s_query, t_query, out_query, None))
+    lines = []
+    for i, (source, left, lv, m_here, move, total, out_ref, turn_at) in enumerate(plans):
+        gather = Gather(place, *source, lands[i], me_s.at[i], me_r.at[i], g_loc.at[i], tokens)
+        sems = (c_s.at[i], c_r.at[i], e_s.at[i], e_r.at[i], e_l.at[i])
+        lines.append(
+            Line(place, nz, blk, gather, lands[i], left, lv, m_here, move, gots[i], total, out_ref, turn_at, sems, work)
+        )
+    down_a, down_b, down_c, gate_a, gate_b, up_a, up_b, out, query = lines
     lefts = [
-        Plane(place, split, land, le_s.at[i], le_r.at[i], loc.at[25 + i], tokens)
+        Plane(place, split, land, le_s.at[i], le_r.at[i], loc.at[i], tokens)
         for i, (split, land) in enumerate(((left_two, l_two), (err, l_err), (one, l_one)))
     ]
-    work = (mv, lv, acc, stage, work_sem)
-    first_a, first_b = pl.ds(0, cols_a), pl.ds(cols_a, rest_a)
-    lines = [
-        Line(place, nz, blk, *refs, (c_s.at[i], c_r.at[i], e_s.at[i], e_r.at[i], e_l.at[i]), work)
-        for i, refs in enumerate((
-            (m_down_a, left_cot, s_first.at[:, :, first_a], g_down_a, t_first.at[:, first_a], out_down, (turned, cols, 0)),
-            (m_down_b, left_cot, s_first.at[:, :, first_b], g_down_b, t_first.at[:, first_b], out_down, (turned, cols, cols_a)),
-            (m_gate, l_two, s_second, g_gate, t_second, out_gate, (turned, cols, 0)),
-            (m_up, l_two, s_first, g_up, t_first, out_up, (turned, cols, 0)),
-            (m_out, l_err, s_out, g_out, t_out, out_out, None),
-            (m_query, l_one, s_query, g_query, t_query, out_query, None),
-        ))
-    ]
-    down_a, down_b, gate, up, out, query = lines
 
     for copy in loads[:2]:
         copy.wait()
@@ -693,15 +711,23 @@
             else:
                 ref[:, pl.ds(pl.multiple_of(at, LANE), size)] = now
 
-    first_pass.run(0, 2 * (cols_a // size), units)
-    gathers[0].start()
-    first_pass.run(2 * (cols_a // size), first_pass.regular, units)
+    done_a, done_b = (2 * ((first + wide) // size) for _, first, wide in cuts[:2])
+    first_pass.run(0, done_a, units)
+    down_a.gather.start()
+    first_pass.run(done_a, done_b, units)
+    down_b.gather.start()
+    down_a.load(True)
+    down_a.from_end()
+    first_pass.run(done_b, first_pass.regular, units)
     second_pass.begin()
     first_pass.end(units)
-    gathers[1].start()
+    down_c.gather.start()
     lefts[0].start()
     for copy in loads[2:]:
         copy.start()
+    down_b.load()
+    down_b.from_end()
+    down_a.between(0, 2)
 
     def block_of(ref, at):
         if at is None:
@@ -734,16 +760,60 @@
         for zy in range(n // 2):
             to = wbuf.at[4 * k + zy // 2, :, (zy % 2) * half : (zy % 2 + 1) * half]
             load_square.append(pltpu.make_async_copy(ref.at[zy * blk : (zy + 1) * blk, :], to, o_sem.at[k, zy]))
-    for copy in load_square:
+    for copy in load_square[: n // 2]:
         copy.start()
 
     def square_block(k, zy):
         return wbuf[4 * k + zy // 2, :, (zy % 2) * half : (zy % 2 + 1) * half]
 
-    gathers[0].wait()
-    down_a.load(True)
-    down_a.steps()
-    down_a.own_block()
+    gate_a.gather.start()
+    down_a.between(2, 3)
+    down_b.between(0, 2)
+    down_c.load()
+    down_c.from_end()
+
+    third_pass.begin()
+    sums[...] = jnp.zeros_like(sums)
+
+    def out_units(slots, at):
+        add_up([(block_of(hidden, at), slots[0])])
+
+    third_pass.run(0, third_pass.regular, out_units)
+    third_pass.end(out_units)
+    for db in range(width // size):
+        mixed[:, db * size : (db + 1) * size] = sums[db * tokens : (db + 1) * tokens, :].astype(BF)
+    ffn_copy = remote(mixed.at[:, aligned(1 - t, half)], ffn_in, tp_s.at[4], tp_r.at[4], place.twin)
+    ffn_copy.start()
+    ffn_keep = pltpu.make_async_copy(mixed.at[:, mine], ffn_own, loc.at[6])
+    ffn_keep.start()
+    for copy in load_square[n // 2 :]:
+        copy.start()
+    down_b.between(2, 3)
+
+    for copy in loads[3:]:
+        copy.wait()
+
+    def first_norm(j, unused):
+        at = aligned(j, fine)
+        x = x_all[at, :].astype(F32)
+        root = lax.rsqrt(jnp.mean(x * x, axis=-1, keepdims=True) + EPSILON)
+        low = (x * root * gain_one[...]).astype(BF)
+        for zy in range(n // 2):
+            zz, yy = divmod(zy, 2)
+            one[yy, at, zz * blk : (zz + 1) * blk] = low[:, zy * blk : (zy + 1) * blk]
+        return unused
+
+    lax.fori_loop(0, tokens // fine, first_norm, 0)
+    attention_masks(seg_all, seg_row, seg_col, n, tok)
+
+    def turn(i, unused):
+        at = aligned(i, tok)
+        k_t[:, at] = jnp.transpose(uk[at, :].astype(F32)).astype(BF)
+        return unused
+
+    lax.fori_loop(0, n, turn, 0)
+    sums[...] = jnp.zeros_like(sums)
+    down_c.between(0, 2)
 
     spread_att = Spread(
         place,
@@ -796,60 +866,13 @@
         for g in range(2)
     ]
     spread_gain[0].start()
+    gate_b.gather.start()
     lefts[0].forward()
-    gathers[2].start()
-    gathers[3].start()
-    lefts[1].start()
-    gathers[4].start()
-
-    gathers[1].wait()
-    down_b.load(False)
-    at_end = (z == 0) | (z == nz - 1)
-
-    @pl.when(at_end)
-    def _():
-        down_b.steps()
-
-    down_b.own_block()
-
-    third_pass.begin()
-    sums[...] = jnp.zeros_like(sums)
-
-    def out_units(slots, at):
-        add_up([(block_of(hidden, at), slots[0])])
-
-    third_pass.run(0, third_pass.regular, out_units)
-    third_pass.end(out_units)
-    for db in range(width // size):
-        mixed[:, db * size : (db + 1) * size] = sums[db * tokens : (db + 1) * tokens, :].astype(BF)
-    ffn_copy = remote(mixed.at[:, aligned(1 - t, half)], ffn_in, tp_s.at[4], tp_r.at[4], place.twin)
-    ffn_copy.start()
-    ffn_keep = pltpu.make_async_copy(mixed.at[:, mine], ffn_own, loc.at[6])
-    ffn_keep.start()
-
-    for copy in loads[3:]:
-        copy.wait()
-
-    def first_norm(j, unused):
-        at = aligned(j, fine)
-        x = x_all[at, :].astype(F32)
-        root = lax.rsqrt(jnp.mean(x * x, axis=-1, keepdims=True) + EPSILON)
-        low = (x * root * gain_one[...]).astype(BF)
-        for zy in range(n // 2):
-            zz, yy = divmod(zy, 2)
-            one[yy, at, zz * blk : (zz + 1) * blk] = low[:, zy * blk : (zy + 1) * blk]
-        return unused
-
-    lax.fori_loop(0, tokens // fine, first_norm, 0)
-    attention_masks(seg_all, seg_row, seg_col, n, tok)
-
-    def turn(i, unused):
-        at = aligned(i, tok)
-        k_t[:, at] = jnp.transpose(uk[at, :].astype(F32)).astype(BF)
-        return unused
-
-    lax.fori_loop(0, n, turn, 0)
-    sums[...] = jnp.zeros_like(sums)
+
+    down_c.between(2, 3)
+    lefts[0].finish()
+    gate_a.load(True)
+    gate_a.from_end()
 
     spread_att.wait()
 
@@ -892,31 +915,24 @@
         lax.fori_loop(qi * owners, (qi + 1) * owners, spread_dq.start_to, 0)
         udk[qat, :] = sums[qat, :HEAD_DIM].astype(BF)
         udv[qat, :] = sums[qat, HEAD_DIM:].astype(BF)
-        lax.fori_loop(qi * owners, (qi + 1) * owners, spread_dk.start_to, 0)
-        lax.fori_loop(qi * owners, (qi + 1) * owners, spread_dv.start_to, 0)
         return unused
 
     lax.fori_loop(0, length // block, query_step, 0)
 
-    @pl.when(jnp.logical_not(at_end))
-    def _():
-        down_b.steps()
-
+    up_a.gather.start()
+    up_b.gather.start()
+    gate_a.between(0, 2)
+    gate_b.load()
+    gate_b.from_end()
+    gate_a.between(2, 3)
+    gate_b.between(0, 2)
     down_a.finish()
-    gathers[2].wait()
-    lefts[0].finish()
-    gate.load(True)
-    gate.steps()
-    gate.own_block()
-    down_a.left_here()
     down_b.finish()
+    down_c.finish()
 
     for copy in load_square[n // 2 :]:
         copy.wait()
     spread_dq.wait()
-    gathers[5].start()
-    lefts[2].start()
-    lefts[1].forward()
 
     def one_copy(i):
         at = aligned(i, chunk)
@@ -932,12 +948,16 @@
 
     lax.fori_loop(0, 4, back_query, 0)
 
-    gathers[3].wait()
-    down_a.sent()
-    down_b.sent()
-    up.load(False)
-    up.steps()
-    up.own_block()
+    gate_b.between(2, 3)
+    for line in (down_a, down_b, down_c):
+        line.sent()
+    up_a.load()
+    up_a.from_end()
+    up_a.between(0, 2)
+    lefts[1].start()
+    out.gather.start()
+    lefts[2].start()
+    query.gather.start()
 
     def last_norm(i, gain_sum):
         one_copy(i).wait()
@@ -963,22 +983,32 @@
     give = pltpu.make_async_copy(mid.at[:, mine], input_grad, loc.at[24])
     give.start()
 
-    gathers[4].wait()
+    up_b.load()
+    up_b.from_end()
+    spread_dk.start()
+    spread_dv.start()
+    up_a.between(2, 3)
+    up_b.between(0, 2)
+    for line in (down_a, down_b, down_c):
+        line.left_here()
+    gate_a.finish()
+    gate_b.finish()
+    lefts[1].forward()
     lefts[1].finish()
+    out.load(True)
+    out.from_end()
+    up_b.between(2, 3)
+    out.between(0, 2)
     lefts[2].forward()
-    out.load(True)
-    out.steps()
-    out.own_block()
-
-    gathers[5].wait()
     lefts[2].finish()
     query.load(True)
-    query.steps()
-    query.own_block()
-    down_b.left_here()
-    gate.finish()
-    gate.left_here()
-    up.finish()
+    query.from_end()
+    out.between(2, 3)
+    query.between(0, 3)
+    for line in (gate_a, gate_b):
+        line.left_here()
+    up_a.finish()
+    up_b.finish()
     out.finish()
     query.finish()
 
@@ -990,9 +1020,9 @@
     ffn_copy.wait()
     ffn_keep.wait()
     give.wait()
-    for line in lines[2:]:
+    for line in lines[3:]:
         line.sent()
-    for line in lines[3:]:
+    for line in lines[5:]:
         line.left_here()
     for line in lines:
         line.arrived()
@@ -1006,12 +1036,16 @@
     ff = wg.shape[0]
     size = 2 * LANE
     cols = -(-ff // size) * LANE
-    cols_a = cols // size * size // 2 // size * size + (size if cols // size % 2 else 0)
-    sizes = (ff, cols, cols_a)
+    firsts = (0, size, 3 * size, cols)
+    thirds = [(firsts[i], firsts[i + 1] - firsts[i]) for i in range(3)]
+    halves = [(0, firsts[2]), (firsts[2], cols - firsts[2])]
+    cuts = tuple((kind, *cut) for kind, parts in (("down", thirds), ("gate", halves), ("up", halves)) for cut in parts)
+    sizes = (ff, cols, cuts)
     x_all, cot_all, left_cot, middle, normed_two, left_two, attended, uq, uk, uv, uo, lse, seg_all = forward
     dma = pltpu.SemaphoreType.DMA
     anywhere, here = pl.BlockSpec(memory_space=pl.ANY), pl.BlockSpec(memory_space=pltpu.VMEM)
-    wide = (cols_a, cols - cols_a, cols, cols, half // 2, half // 2)
+    wide = (*(w for _, _, w in cuts), half // 2, half // 2)
+    kept = (cols, cols, half // 2, half // 2)
     outs = [
         (vm((tokens, half), BF), anywhere),
         (vm((tokens, half), BF), anywhere),
@@ -1042,13 +1076,15 @@
         pltpu.VMEM((length, LANE), F32), pltpu.VMEM((HEAD_DIM, length), BF), line,
         unit, unit, unit, pltpu.VMEM((tokens, half), BF),
         pltpu.VMEM((2, n, 1, width // n), F32), pltpu.VMEM((2, n, 1, width // n), F32),
-        *(pltpu.VMEM((nz - 1, blk, c), BF) for c in wide[2:]),
-        *(pltpu.VMEM((blk, c), F32) for c in wide[2:]),
+        *(pltpu.VMEM((nz - 1, blk, c), BF) for c in kept),
+        *(pltpu.VMEM((blk, c), F32) for c in kept),
         pltpu.VMEM((cols, blk), F32),
-        pltpu.VMEM((PLANE * tokens, cols), BF), pltpu.VMEM((PLANE * tokens, width // 2), BF),
+        pltpu.VMEM((PLANE * tokens, cols), BF), *(pltpu.VMEM((PLANE * tokens, half // 2), BF) for _ in range(2)),
+        *(pltpu.VMEM((PLANE * tokens, width // 2), BF) for _ in range(2)),
         pltpu.VMEM((blk, cols), F32), pltpu.VMEM((blk, cols), BF),
-        dma((9,)), dma((9,)), dma((6, n)), dma((6, n)), dma((6, 3)), dma((6, 3)), dma((3, 3)), dma((3, 3)),
-        dma((6, nz - 1)), dma((6, nz + 1)), dma((6,)), dma((6,)), dma((6,)), dma((28,)), dma((3,)),
+        dma((9,)), dma((9,)), dma((6, n)), dma((6, n)), dma((len(wide), 3)), dma((len(wide), 3)), dma((3, 3)), dma((3, 3)),
+        dma((len(wide), nz - 1)), dma((len(wide), nz + 1)), *(dma((len(wide),)) for _ in range(3)), dma((28,)),
+        dma((len(wide),)), dma((3,)),
         dma((3, 2, 3)), dma((3, 2, 3)), dma((2, n // 2)),
     ]
     return pl.pallas_call(

time: 377 us -> 351 us (0.931)
  Pallas kernels: 357 us -> 335 us
    pallas_call x1, Pallas kernels: 277 us -> 254 us  [backward_part(): pl.pallas_call(functools.partial(backward_kernel, geo, sizes), out_shape=...]
where the time goes in v3:
time: 351 us; the launch traced here: 349 us
  Pallas kernels  335 us (95%)
  local copies, waits for them, and re-layouts  7.11 us (2%)
  other arithmetic  6.45 us (2%)
    pallas_call x1, Pallas kernels, backward_part(): pl.pallas_call(functools.partial(backward_kernel, geo, sizes), out_shape=...  254 us
    pallas_call x1, Pallas kernels, forward_part(): pl.pallas_call(functools.partial(forward_kernel, geo), out_shape=outs, in...  80.5 us

profile of v3, /device:TPU:0, one launch (start us, length us, event | category | flops | bytes accessed | tf_op | source)
XLA Modules:
  0.0 349.0 jit_solution(8349677410397857850)
XLA Ops:
  0.6 1.2 convert_element_type.14
  1.9 80.5 %attention_forward.1 = (bf16[256,2048]{1,0:T(8,128)(2,1)}, bf16[256,2048]{1,0:T(8,128)(2,1)}, bf16[1024,1024]{1,0:T(8,128)(2,1)}, f32[256,2048]{1,0:T(8,128)}, b...) custom-call(bf16[256,1024]{1,0:T(8,128)(2,1)} %bitcast.33, ...), custom_call_target="tpu_custom_call" | custom-call | tf_op jit(solution)/shard_map/attention_forward/pallas_call | solution.py:366
  82.4 254.2 %feed_forward_and_backward.1 = (bf16[256,1024]{1,0:T(8,128)(2,1)}, bf16[256,1024]{1,0:T(8,128)(2,1)}, f32[256,1024]{1,0:T(8,128)}, bf16[256,1024]{1,0:T(8,128)(2...) custom-call(bf16[2752,2048]{1,0:T(8,128)(2,1)} %bitcast.26, ...), custom_call_target="tpu_custom_call" | custom-call | tf_op jit(solution)/shard_map/feed_forward_and_backward/pallas_call | solution.py:1090
  336.6 0.0 copy-start.1
  336.6 3.6 %slice_bitcast_fusion = (f32[128,2752]{0,1:T(8,128)}, f32[128,2752]{0,1:T(8,128)}) fusion(f32[2816,128]{1,0:T(8,128)} %get-tuple-element.58, f32[2816,128]{1,0:T(8,128)} %get-tuple-element.57), kind=kLoop, calls=%fused_computation | loop fusion | bytes 5636096 | tf_op jit(solution)/shard_map/transpose | solution.py:1141
  340.2 0.0 copy-start.4
  340.3 0.0 copy-done.1
  340.3 0.0 copy-start.3
  340.3 1.2 slice_bitcast_fusion.2
  341.4 0.0 copy-done.4
  341.4 0.0 copy-start
  341.4 0.0 copy-start.7
  341.4 1.1 convert.2
  342.5 0.0 copy-done.3
  342.5 1.1 convert.3
  343.6 0.0 copy-start.6
  343.6 0.0 copy-done
  343.6 0.0 copy-done.7
  343.6 0.0 copy-start.8
  343.6 0.0 copy-start.2
  343.6 2.2 add_convert_fusion
  345.8 0.0 copy-done.6
  345.8 0.0 copy-start.5
  345.8 0.8 broadcast_multiply_fusion
  346.7 0.0 copy-done.8
  346.7 0.5 slice_bitcast_fusion.3
  347.2 0.0 copy-done.2
  347.2 1.0 copy.25
  348.2 0.0 copy-done.5
  348.2 0.8 copy.26
Async XLA Ops:
  336.6 3.6 %copy-start.1 = (f32[2816,128]{1,0:T(8,128)S(1)}, f32[2816,128]{1,0:T(8,128)}, u32[]{:S(2)}) copy-start(f32[2816,128]{1,0:T(8,128)} %get-tuple-element.56) | copy-start | bytes 4325380
  340.2 1.2 copy-start.4
  340.3 2.3 copy-start.3
  341.4 2.2 copy-start
  341.4 2.2 copy-start.7
  343.6 2.2 copy-start.6
  343.6 3.1 copy-start.8
  343.6 3.6 %copy-start.2 = (f32[256,1024]{1,0:T(8,128)S(1)}, f32[256,1024]{1,0:T(8,128)}, u32[]{:S(2)}) copy-start(f32[256,1024]{1,0:T(8,128)} %get-tuple-element.50) | copy-start | bytes 3145732
  345.8 2.3 copy-start.5
